TPU v7x, 32 devices: a whole 2x2x4 slice. The times are simulated.
32 devices in a mesh: dp: 4 (over y, x), row: 2 (over core), col: 4 (over z).
Axes of the slice: x: 2, y: 2, z: 4, core: 2. Of those that a mesh axis runs over, the one named last changes fastest.
Arguments:
- tokens: bfloat16 [64, 196, 1280], P(('dp', 'row', 'col')), may hold values from -72 to 72
- valid_mask: int32 [64, 196], P(('dp', 'row', 'col')), may hold values from 0 to 1, as said below
- out_grad: bfloat16 [64, 196, 1280], P(('dp', 'row', 'col')), may hold values from -6 to 6
- first_gain: float32 [1280], replicated, may hold values from 0.5 to 1.5
- first_shift: float32 [1280], replicated, may hold values from -1 to 1
- qkv_weight: bfloat16 [1280, 3, 1280], P('row', None, 'col'), may hold values from -1 to 1
- qkv_bias: float32 [2, 1280], P(None, 'col'), may hold values from -1 to 1
- rel_height: float32 [27, 80], replicated, may hold values from -0.9 to 0.9
- rel_width: float32 [27, 80], replicated, may hold values from -0.9 to 0.9
- proj_weight: bfloat16 [1280, 1280], P('col', 'row'), may hold values from -0.625 to 0.625
- proj_bias: float32 [1280], replicated, may hold values from -1 to 1
- second_gain: float32 [1280], replicated, may hold values from 0.5 to 1.5
- second_shift: float32 [1280], replicated, may hold values from -1 to 1
- expand_weight: bfloat16 [1280, 5120], P('row', 'col'), may hold values from -1 to 1
- expand_bias: float32 [5120], P('col'), may hold values from -1 to 1
- shrink_weight: bfloat16 [5120, 1280], P('col', 'row'), may hold values from -0.078125 to 0.078125
- shrink_bias: float32 [1280], replicated, may hold values from -1 to 1
Outputs:
- block_out: bfloat16 [64, 196, 1280], P(('dp', 'row', 'col'))
- input_grad: float32 [64, 196, 1280], P(('dp', 'row', 'col'))
- first_gain_grad: float32 [1280], replicated
- first_shift_grad: float32 [1280], replicated
- qkv_weight_grad: float32 [1280, 3, 1280], P('row', None, 'col')
- qkv_bias_grad: float32 [2, 1280], P(None, 'col')
- rel_height_grad: float32 [27, 80], replicated
- rel_width_grad: float32 [27, 80], replicated
- proj_weight_grad: float32 [1280, 1280], P('col', 'row')
- proj_bias_grad: float32 [1280], replicated
- second_gain_grad: float32 [1280], replicated
- second_shift_grad: float32 [1280], replicated
- expand_weight_grad: float32 [1280, 5120], P('row', 'col')
- expand_bias_grad: float32 [5120], P('col')
- shrink_weight_grad: float32 [5120, 1280], P('col', 'row')
- shrink_bias_grad: float32 [1280], replicated
- rms: float32 [5], replicated
Inputs may be any that keep to these rules, and one draw needn't show every extreme that they name: `valid_mask`: windows come 25 to an image, 5 by 5 windows of 14 by 14 tokens in row-major order, the last image possibly incomplete; 1 marks tokens inside the image content, a rectangle at the top left that is 64 tokens along one side and at least half of that along the other.
All inputs are finite; a program needn't handle non-finite values.
Results may differ from a plain program's by a relative error of at most 0.012.
Values may be sent and summed in bfloat16 or wider, within the bound.
A program may use at most 256 MiB of HBM per device.

v0:
```python
import functools

import jax
import jax.numpy as jnp
import numpy as np
from jax import lax
from jax.experimental import pallas as pl
from jax.experimental.pallas import tpu as pltpu
from jax.sharding import PartitionSpec as P

BF = jnp.bfloat16
F32 = jnp.float32
LANES = 128
SIDE = 14
SIDE_PAD = 16
WROWS = SIDE * SIDE_PAD
HEAD = 80
AT_H = HEAD
AT_W = HEAD + SIDE
AT_MASK = HEAD + 2 * SIDE
COL_W = 64


def dot(a, b):
    return jnp.dot(a, b, preferred_element_type=F32)


def dot_nt(a, b):
    return lax.dot_general(a, b, (((1,), (1,)), ((), ())), preferred_element_type=F32)


def dot_tn(a, b):
    return lax.dot_general(a, b, (((0,), (0,)), ((), ())), preferred_element_type=F32)


def lane_ids():
    return lax.broadcasted_iota(jnp.int32, (WROWS, LANES), 1)


def row_ids():
    return lax.broadcasted_iota(jnp.int32, (WROWS, LANES), 0)


def key_codes():
    u = np.arange(WROWS)[:, None]
    lane = np.arange(LANES)[None, :]
    k, l = u // SIDE_PAD, u % SIDE_PAD
    height = lane - AT_H == k
    width = (lane - AT_W == l) & (l < SIDE)
    width_back = (AT_W + SIDE - 1 - lane == l) & (l < SIDE)
    plain = np.where(height | width, 1.0, 0.0)
    masked = np.where((lane == AT_MASK) & (l >= SIDE), -1e30, plain)
    back = np.where(height | width_back, 1.0, 0.0)
    return np.stack([masked, plain, back]).astype(BF)


def split_low(values):
    high = values.astype(BF)
    return high, (values - high.astype(F32)).astype(BF)


def relative_tables(rel_h, rel_w, rel_query, rel_back):
    count, rows = 2 * SIDE - 1, rel_h.shape[0]
    offset = lax.broadcasted_iota(jnp.int32, (rows, LANES), 0)
    lane = lax.broadcasted_iota(jnp.int32, (rows, LANES), 1)

    def places(first, step):
        return jnp.where((lane == first + step * offset) & (offset < count), 1.0, 0.0).astype(BF)

    heights, widths = places(count - 1, -1), places(COL_W + count - 1, -1)
    widths_back = places(COL_W, 1)
    tall, wide = rel_h[...], rel_w[...]
    rel_query[...] = jnp.zeros_like(rel_query)
    rel_back[...] = jnp.zeros_like(rel_back)
    for part, (a, b) in enumerate(zip(split_low(tall * HEAD**0.5), split_low(wide * HEAD**0.5))):
        at = part * LANES
        rel_query[at : at + HEAD] = (dot_tn(a, heights) + dot_tn(b, widths)).astype(BF)
    for part, (a, b) in enumerate(zip(split_low(tall), split_low(wide))):
        table = (dot_tn(heights, a) + dot_tn(widths_back, b)).astype(BF)
        for place in ((0, 1), (2,))[part]:
            rel_back[place * LANES : (place + 1) * LANES, :HEAD] = table


def query_codes(query, rel_query):
    full = dot(jnp.concatenate([query, query], axis=1), rel_query)
    tiles = full.reshape(SIDE, SIDE_PAD, LANES)
    heights = jnp.concatenate(
        [pltpu.roll(tiles[i], AT_H - (SIDE - 1 - i), 1) for i in range(SIDE)], axis=0
    )
    widths = pltpu.roll(
        tiles, AT_W - COL_W - (SIDE - 1), 2, stride=1, stride_axis=1
    ).reshape(WROWS, LANES)
    lane = lane_ids()
    codes = jnp.where(
        (lane >= AT_H) & (lane < AT_W),
        heights,
        jnp.where((lane >= AT_W) & (lane < AT_MASK), widths, 0.0),
    )
    high, rest = split_low(codes)
    first = query + high + jnp.where(lane == AT_MASK, 1.0, 0.0).astype(BF)
    return jnp.concatenate([first, rest], axis=1)


def softmax_rows(query, key, rel_query, codes_ref):
    left = query_codes(query, rel_query)
    right = jnp.concatenate([key + codes_ref[0], codes_ref[1]], axis=1)
    scores = dot_nt(left, right)
    top = jnp.max(scores, axis=1, keepdims=True)
    weights = jnp.exp((scores - top) * (HEAD**-0.5))
    return weights / jnp.sum(weights, axis=1, keepdims=True)


def attend(query, key, value, rel_query, codes_ref):
    probs = softmax_rows(query, key, rel_query, codes_ref)
    return dot(probs.astype(BF), value)


def attend_back(query, key, value, grad, rel_query, rel_back, codes_ref):
    probs = softmax_rows(query, key, rel_query, codes_ref)
    prob_grad = dot_nt(grad, value)
    inner = jnp.sum(probs * prob_grad, axis=1, keepdims=True)
    score_low = (probs * (prob_grad - inner)).astype(BF)
    value_grad = dot_tn(probs.astype(BF), grad)
    key_grad = dot_tn(score_low, query) * (HEAD**-0.5)
    mixed = dot(score_low, key + codes_ref[2])
    tiles = mixed.reshape(SIDE, SIDE_PAD, LANES)
    heights = jnp.concatenate(
        [pltpu.roll(tiles[i], (SIDE - 1 - i - AT_H) % LANES, 1) for i in range(SIDE)], axis=0
    )
    widths = pltpu.roll(
        tiles, (COL_W - AT_W) % LANES, 2, stride=1, stride_axis=1
    ).reshape(WROWS, LANES)
    lane, row = lane_ids(), row_ids()
    first_h = SIDE - 1 - row // SIDE_PAD
    first_w = COL_W + row % SIDE_PAD
    offsets = jnp.where(
        (lane >= first_h) & (lane < first_h + SIDE),
        heights,
        jnp.where((lane >= first_w) & (lane < first_w + SIDE), widths, 0.0),
    )
    high, rest = split_low(offsets)
    query_grad = jnp.where(lane < HEAD, mixed, 0.0) * (HEAD**-0.5) + dot(
        jnp.concatenate([high, rest, high], axis=1), rel_back
    )
    rel_grad = dot_tn(jnp.concatenate([high, rest], axis=1), query)
    return query_grad, key_grad, value_grad, rel_grad


def pad_head(piece):
    return jnp.concatenate([piece, jnp.zeros((piece.shape[0], LANES - HEAD), piece.dtype)], axis=1)


def qkv_low(s, rows, h1, wq, bias, half):
    return (dot_nt(h1[rows, :half], block(wq, s, 0)) + dot_nt(h1[rows, half:], block(wq, s, 1)) + bias).astype(BF)


def head_of(low, part, heads, hh):
    at = (part * heads + hh) * HEAD
    return pad_head(low[:, at : at + HEAD])


def attention_slab(s, h1, wq, wp, bias, rel_query, codes, attended, total, heads, half, half_done):
    count = h1.shape[0] // WROWS

    @pl.loop(0, count)
    def _(m):
        rows = pl.ds(pl.multiple_of((m + count // 2) % count * WROWS, WROWS), WROWS)
        low = qkv_low(s, rows, h1, wq, bias, half)
        outs = []
        for hh in range(heads):
            query, key, value = (head_of(low, part, heads, hh) for part in range(3))
            outs.append(attend(query, key, value, rel_query[...], codes)[:, :HEAD])
        out_low = jnp.concatenate(outs, axis=1).astype(BF)
        attended[s, rows] = out_low
        total[rows, :half] += dot(out_low, block(wp, s, 0))
        total[rows, half:] += dot(out_low, block(wp, s, 1))

        @pl.when(m == count // 2 - 1)
        def _():
            half_done()


SQRT_HALF = 0.5**0.5
PDF_SCALE = 0.3989422804014327


def mlp_rows(s, place, m, h2, gm, we, ws, bias, act, gpre, total, back, bias_grad, half):
    count = h2.shape[0] // 2

    @pl.loop(0, 1)
    def _(step):
        rows = pl.ds(pl.multiple_of((m + step) * count, count), count)
        pre = dot(h2[rows, :half], block(we, place, 0)) + dot(h2[rows, half:], block(we, place, 1)) + bias
        cdf = 0.5 + 0.5 * lax.erf(pre * SQRT_HALF)
        slope = cdf + pre * (PDF_SCALE * jnp.exp(-0.5 * pre * pre))
        act_low = (pre * cdf).astype(BF)
        act[rows, :] = act_low
        hidden = dot_nt(gm[rows, :half], block(ws, place, 0)) + dot_nt(gm[rows, half:], block(ws, place, 1))
        gpre_low = (hidden * slope).astype(BF)
        gpre[rows, :] = gpre_low
        bias_grad[s] += jnp.sum(gpre_low.astype(F32), axis=0, keepdims=True)
        total[rows, :half] += dot(act_low, block(ws, place, 0))
        total[rows, half:] += dot(act_low, block(ws, place, 1))
        back[rows, :half] += dot_nt(gpre_low, block(we, place, 0))
        back[rows, half:] += dot_nt(gpre_low, block(we, place, 1))


def attention_back_slab(
    s, h1, ga, wq, wp, bias, rel_query, rel_back, codes, gqkv, back, bias_grad, rel_grad, heads, half, half_done
):
    count = h1.shape[0] // WROWS

    @pl.loop(0, count)
    def _(m):
        rows = pl.ds(pl.multiple_of((m + count // 2) % count * WROWS, WROWS), WROWS)
        low = qkv_low(s, rows, h1, wq, bias, half)
        grad = (dot_nt(ga[rows, :half], block(wp, s, 0)) + dot_nt(ga[rows, half:], block(wp, s, 1))).astype(BF)
        parts = [[], [], []]
        for hh in range(heads):
            query, key, value = (head_of(low, part, heads, hh) for part in range(3))
            got = attend_back(
                query, key, value, head_of(grad, 0, heads, hh), rel_query[...], rel_back[...], codes
            )
            for part in range(3):
                parts[part].append(got[part][:, :HEAD])
            rel_grad[...] += got[3]
        grad_low = jnp.concatenate(parts[0] + parts[1] + parts[2], axis=1).astype(BF)
        gqkv[rows, : grad_low.shape[1]] = grad_low
        bias_grad[s] += jnp.sum(grad_low.astype(F32), axis=0, keepdims=True)
        back[rows, :half] += dot(grad_low, block(wq, s, 0))
        back[rows, half:] += dot(grad_low, block(wq, s, 1))

        @pl.when(m == count // 2 - 1)
        def _():
            half_done()


MESH_ID = pl.DeviceIdType.MESH
ARRAYS = ("qkv", "proj", "expand", "shrink")
CHUNK = 64
EPS = 1e-06
SPARE = 4


def halves(rows):
    first = (rows // 2 + 15) // 16 * 16
    return first, rows - first


def flip(index, k):
    return ((index // 2 + k // 2) % 2) * 2 + (index % 2 + k % 2) % 2


def block(ref, slab, half):
    value = ref[slab, half]
    return value.reshape(value.shape[0] * value.shape[1], value.shape[2])


def add_low(target, index, extra):
    target[index] = (target[index].astype(F32) + extra.astype(F32)).astype(BF)


def kernel(
    tokens_in, mask_in, out_grad_in, gain_one_in, shift_one_in, gain_two_in, shift_two_in, proj_bias_in, shrink_bias_in,
    qkv_bias_in, expand_bias_in, rel_h_in, rel_w_in, codes, qkv_src, proj_src, expand_src, shrink_src,
    block_out, input_grad, qkv_out, proj_out, expand_out, shrink_out, early_out, late_out, rel_out,
    rxq, rxp, rxe, rxs, ryq, ryp, rye, rys, rx2q, rx2p, rx2e, rx2s, ry2q, ry2p, ry2e, ry2s, rzq, rzp, rze, rzs, pair_back, pair_out,
    wq, wp, we, ws, tokens, keep, h1, grads, normed, got_low, attended, total, back, xr, xr2, middle, act, gpre,
    bias_all, early, early_got, late, late_got, rel, rel_got, bias_e, bias_q, rel_acc, rel_query, rel_back, rel_pad,
    gsend, grecv, rsend, rrecv, fsend, frecv, csend, crecv, zsend, zrecv, qsend, qrecv, local, qlocal,
):
    d, r, z = lax.axis_index("dp"), lax.axis_index("row"), lax.axis_index("col")
    h, b = d // 2, d % 2
    own = tokens.shape[0]
    width = tokens.shape[1]
    half = width // 2
    heads = 2
    bufs = (wq, wp, we, ws)
    outs = (qkv_out, proj_out, expand_out, shrink_out)
    rx, ry = (rxq, rxp, rxe, rxs), (ryq, ryp, rye, rys)
    rx2, ry2 = (rx2q, rx2p, rx2e, rx2s), (ry2q, ry2p, ry2e, ry2s)
    rz = (rzq, rzp, rze, rzs)
    parts = [halves(buf.shape[3]) for buf in bufs]
    attn, mlp = (0, 1), (2, 3)
    qkv_width = 3 * attended.shape[2]

    along_x = (h * 2 + 1 - b, r, z)
    along_y = ((1 - h) * 2 + b, r, z)
    across = ((1 - h) * 2 + 1 - b, r, z)
    partner = (d, 1 - r, z)
    pair, remote_slab = (d, r, flip(z, 1)), flip(z, 2)
    gm, gmz, h2, h2z = grads.at[0], grads.at[1], normed.at[0], normed.at[1]

    def along_z(k):
        return (d, r, flip(z, k))

    def remote(src, dst, sems, recvs, index, device, got=None):
        return pltpu.make_async_remote_copy(
            src_ref=src,
            dst_ref=dst,
            send_sem=sems.at[index],
            recv_sem=recvs.at[index if got is None else got],
            device_id=device,
            device_id_type=MESH_ID,
        )

    up = z // 2
    is_end = (z + 1) // 2 % 2 == 0
    is_inner = (z + 1) // 2 % 2 == 1

    def slab_of(i):
        far = i // 2
        return (1 - far) * flip(z, i) + far * ((1 - up) * i + up * (3 - i))

    def first_part(a):
        return pl.ds(0, parts[a][0])

    def second_part(a):
        return pl.ds(parts[a][0], parts[a][1])

    def gather_z(a, s, step):
        at = bufs[a].at[s, h, b]
        return remote(at, at, gsend, grecv, (a, s, 0 if step < 0 else 5), (d, r, z + step), (a, s, 0))

    def gather_far(a):
        return remote(bufs[a].at[0, h, b], bufs[a].at[1, h, b], gsend, grecv, (a, 0, 0), (d, r, remote_slab))

    def ring(a, slab, sends, recvs, index, kind, arriving):
        buf = bufs[a]
        if kind == 1:
            at, device = (buf.at[slab, h, 1 - b] if arriving else buf.at[slab, h, b]), along_x
        elif kind == 2:
            at, device = (buf.at[slab, 1 - h, b] if arriving else buf.at[slab, h, b]), along_y
        elif kind == 3:
            at = buf.at[slab, 1 - h if arriving else h, 1 - b, first_part(a)]
            device = along_y
        else:
            at = buf.at[slab, 1 - h, 1 - b if arriving else b, second_part(a)]
            device = along_x
        return remote(at, at, sends, recvs, index, device)

    def gather(a, s, kind, arriving=False):
        return ring(a, s, gsend, grecv, (a, s, kind), kind, arriving)

    def spread(a, kind, arriving=False):
        return ring(a, final_slot(a), fsend, frecv, (a, kind), kind, arriving)

    def sends_along_z(group, s, act_on):
        for a in group:

            @pl.when((s >= z) & (z > 0))
            def _():
                act_on(gather_z(a, s, -1))

            @pl.when((s <= z) & (z < 3))
            def _():
                act_on(gather_z(a, s, 1))

    def start_z(group):
        sends_along_z(group, z, lambda copy: copy.start())

    def relay(group, i):
        s = slab_of(i)
        for a in group:
            gather_z(a, s, 1).wait_recv()
            sends_along_z((a,), s, lambda copy: copy.start())

    def place_of(a, i):
        return slab_of(i) if a in attn else 1

    def share(group, i):
        for a in group:
            gather(a, place_of(a, i), 1).start()
            gather(a, place_of(a, i), 2).start()

    def share_far(group):
        for a in group:
            gather_far(a).wait_recv()
            share((a,), 1)

    def pass_diagonal(group, i):
        for a in group:
            s = place_of(a, i)
            gather(a, s, 1, True).wait_recv()
            gather(a, s, 3).start()
            gather(a, s, 2, True).wait_recv()
            gather(a, s, 4).start()

    def finish_slab(group, i):
        for a in group:
            s = place_of(a, i)
            gather(a, s, 3, True).wait_recv()
            gather(a, s, 4, True).wait_recv()

    def sent_slab(group, i):
        s = slab_of(i)
        sends_along_z(group, s, lambda copy: copy.wait_send())
        for a in group:

            @pl.when(i > 0)
            def _():
                for kind in (1, 2, 3, 4):
                    gather(a, s, kind).wait_send()

    def sent_far(group):
        for a in group:
            gather_far(a).wait_send()
            for kind in (1, 2, 3, 4):
                gather(a, 1, kind).wait_send()

    def step_slab(n):
        return slab_of(3 - n)

    def final_slot(a):
        return z if a in attn else 0

    def slot(a, n):
        if a in mlp:
            return 2 + n
        first = (4 - n) // 4
        return first * SPARE + (1 - first) * step_slab(n - 1 + first)

    def reduce_copy(a, n, kind):
        buf, g = bufs[a], slot(a, n)
        got = None
        if kind == 0:
            src, dst, device = buf.at[g, :, 1 - b, first_part(a)], rx[a].at[n], along_x
        elif kind == 1:
            src, dst, device = buf.at[g, 1 - h, :, second_part(a)], ry[a].at[n], along_y
        elif kind == 2:
            src, dst, device = buf.at[g, 1 - h, b, first_part(a)], ry2[a].at[n], along_y
        elif kind == 3:
            src, dst, device = buf.at[g, h, 1 - b, second_part(a)], rx2[a].at[n], along_x
        elif kind == 4 and a in mlp:
            src, dst, device = buf.at[g, h, b], rz[a].at[0], (d, r, remote_slab)
            got = (a, 0, 4)
        elif kind == 4:
            src, dst, device = buf.at[g, h, b], rz[a].at[z], (d, r, step_slab(n))
            got = (a, z, 4)
        else:
            src, dst, device = buf.at[g, h, b], rz[a].at[5 - n], (d, r, slab_of(1))
            got = (a, 3 - n, 5)
        return remote(src, dst, rsend, rrecv, (a, n, min(kind, 4)), device, got)

    def reduce_z(a, n, act_on):
        if a in mlp:

            @pl.when(n == 1)
            def _():
                act_on(reduce_copy(a, n, 4))

        else:

            @pl.when((n < 3) & (is_inner | (n == 2)))
            def _():
                act_on(reduce_copy(a, n, 4))

            @pl.when(is_end & (n < 2))
            def _():
                act_on(reduce_copy(a, n, 5))

    def reduce_one(group, n):
        for a in group:
            reduce_copy(a, n, 0).start()
            reduce_copy(a, n, 1).start()

    def with_room(body):
        def run(group, n):
            shape = (2 * len(group), 2, halves(max(bufs[a].shape[3] for a in group))[0], half)
            pl.run_scoped(
                lambda room: body(group, n, lambda a, place: room.at[2 * group.index(a) + place]),
                pltpu.VMEM(shape, BF),
            )

        return run

    def reduce_two_body(group, n, scratch):
        loads = []
        for a in group:
            reduce_copy(a, n, 0).wait_recv()
            reduce_copy(a, n, 1).wait_recv()
            for place, got in enumerate((rx[a], ry[a])):
                to = scratch(a, place).at[:, pl.ds(0, parts[a][place])]
                loads.append(pltpu.make_async_copy(got.at[n], to, local.at[a * 2 + place]))
                loads[-1].start()
        for i, a in enumerate(group):
            g = slot(a, n)
            first, second = parts[a]
            loads[2 * i].wait()
            for side in range(2):
                add_low(bufs[a], (g, side, b, first_part(a)), scratch(a, 0)[side, :first])
            reduce_copy(a, n, 2).start()
            loads[2 * i + 1].wait()
            for side in range(2):
                add_low(bufs[a], (g, h, side, second_part(a)), scratch(a, 1)[side, :second])
            reduce_copy(a, n, 3).start()

    def reduce_three_body(group, n, scratch):
        loads = []
        for a in group:
            reduce_copy(a, n, 2).wait_recv()
            reduce_copy(a, n, 3).wait_recv()
            for place, got in enumerate((ry2[a], rx2[a])):
                to = scratch(a, place).at[0, pl.ds(0, parts[a][place])]
                loads.append(pltpu.make_async_copy(got.at[n], to, local.at[a * 2 + place]))
                loads[-1].start()
        for i, a in enumerate(group):
            g = slot(a, n)
            first, second = parts[a]
            loads[2 * i].wait()
            add_low(bufs[a], (g, h, b, first_part(a)), scratch(a, 0)[0, :first])
            loads[2 * i + 1].wait()
            add_low(bufs[a], (g, h, b, second_part(a)), scratch(a, 1)[0, :second])

            @pl.when(is_inner & (n < 2) & (a in attn))
            def _():
                at = rz[a].at[5 - n]
                remote(at, at, rsend, rrecv, (a, n, 4), (d, r, slab_of(1)), (a, 3 - n, 5)).wait_recv()
                pieces = ((0, first, first_part(a)), (1, second, second_part(a)))
                copies = [
                    pltpu.make_async_copy(at.at[part], scratch(a, 0).at[side, pl.ds(0, count)], local.at[a * 2 + side])
                    for side, count, part in pieces
                ]
                for copy in copies:
                    copy.start()
                for copy, (side, count, part) in zip(copies, pieces):
                    copy.wait()
                    add_low(bufs[a], (g, h, b, part), scratch(a, 0)[side, :count])

            reduce_z(a, n, lambda copy: copy.start())

    def reduce_two(group, n):
        with_room(reduce_two_body)(group, n)

    def reduce_three(group, n):
        with_room(reduce_three_body)(group, n)

    def reduce_four(group):
        for a in group:
            rows = bufs[a].shape[3]
            loads = []
            others = ((remote_slab, 0),) if a in mlp else [(slab_of(k), slab_of(k)) for k in (1, 2)]
            for k, (other, place) in enumerate(others, 1):
                at = rz[a].at[place]
                remote(at, at, rsend, rrecv, (a, k, 4), (d, r, other), (a, place, 4)).wait_recv()
                loads.append(pltpu.make_async_copy(at, gpre.at[pl.ds((k - 1) * rows, rows)], local.at[k]))
                loads[-1].start()
            for load in loads:
                load.wait()
            value = bufs[a][slot(a, 0 if a in mlp else 3), h, b].astype(F32)
            for k in range(len(others)):
                value = value + gpre[k * rows : (k + 1) * rows].astype(F32)
            bufs[a][final_slot(a), h, b] = value.astype(BF)
            spread(a, 1).start()
            spread(a, 2).start()

    def reduce_five(group):
        for a in group:
            spread(a, 1, True).wait_recv()
            spread(a, 3).start()
            spread(a, 2, True).wait_recv()
            spread(a, 4).start()

    def qkv_pieces(matrix, side, flat):
        rows = flat.shape[1]
        part = matrix.shape[2]
        cut = rows - part
        return (
            (matrix.at[0, side], flat.at[0, pl.ds(0, part)]),
            (matrix.at[1, side, pl.ds(0, cut)], flat.at[0, pl.ds(part, cut)]),
            (matrix.at[1, side, pl.ds(cut, part - cut)], flat.at[1, pl.ds(0, part - cut)]),
            (matrix.at[2, side], flat.at[1, pl.ds(part - cut, part)]),
        )

    def swap_out(a):
        mine = bufs[a].at[final_slot(a), 1 - r]
        if a == 0:
            pairs = qkv_pieces(outs[a], r, mine)
            return [remote(src, dst, qsend, qrecv, 4 + i, partner) for i, (dst, src) in enumerate(pairs)]
        to = outs[a].at[:, :, half_lanes(r)] if a == 2 else outs[a].at[r]
        return [remote(mine, to, fsend, frecv, (a, 0), partner)]

    def keep_out(a):
        mine = bufs[a].at[final_slot(a), r]
        if a == 0:
            pairs = qkv_pieces(outs[a], r, mine)
            return [pltpu.make_async_copy(src, dst, qlocal.at[i]) for i, (dst, src) in enumerate(pairs)]
        to = outs[a].at[:, :, half_lanes(r)] if a == 2 else outs[a].at[r]
        return [pltpu.make_async_copy(mine, to, local.at[a])]

    def reduce_six(group):
        for a in group:
            spread(a, 3, True).wait_recv()
            spread(a, 4, True).wait_recv()
            for copy in swap_out(a) + keep_out(a):
                copy.start()

    def half_lanes(side):
        return pl.ds(pl.multiple_of(side * half, half), half)

    def exchange(index, src, dst):
        return remote(src, dst, csend, crecv, index, partner)

    rows_own, rows_other = pl.ds(0, own), pl.ds(own, own)
    def source(a, side):
        if a == 2:
            return expand_src.at[:, :, half_lanes(side)]
        return (qkv_src, proj_src, expand_src, shrink_src)[a].at[side]

    def source_swap(a):
        to = bufs[a].at[z if a in attn else 0, r]
        if a == 0:
            pairs = qkv_pieces(qkv_src, 1 - r, to)
            return [remote(src, dst, qsend, qrecv, i, partner) for i, (src, dst) in enumerate(pairs)]
        return [exchange(a, source(a, 1 - r), to)]

    def source_keep(a):
        to = bufs[a].at[z if a in attn else 0, r]
        if a == 0:
            pairs = qkv_pieces(qkv_src, r, to)
            return [pltpu.make_async_copy(src, dst, qlocal.at[i]) for i, (src, dst) in enumerate(pairs)]
        return [pltpu.make_async_copy(source(a, r), to, local.at[a])]

    def start_source(group):
        for a in group:
            for copy in source_swap(a) + source_keep(a):
                copy.start()

    def finish_source(group):
        for a in group:
            for copy in source_swap(a) + source_keep(a):
                copy.wait()

    swap_grad = exchange(4, gm.at[rows_own], gm.at[rows_other])
    swap_h1 = exchange(5, h1.at[rows_own], h1.at[rows_other])
    swap_attn = exchange(6, total.at[rows_other], xr)
    swap_h2 = exchange(7, h2.at[rows_own], h2.at[rows_other])
    swap_mlp = exchange(8, total.at[rows_other], xr)
    swap_gh2 = exchange(9, back.at[rows_other], xr2)
    swap_ga = exchange(10, gm.at[rows_own], gm.at[rows_other])
    swap_gh1 = exchange(11, back.at[rows_other], total.at[rows_other])
    pair_gm = remote(gm.at[rows_own], gmz.at[rows_own], csend, crecv, 12, pair)
    swap_gmz = exchange(13, gmz.at[rows_own], gmz.at[rows_other])
    pair_h2 = remote(h2.at[rows_own], h2z.at[rows_own], csend, crecv, 14, pair)
    swap_h2z = exchange(15, h2z.at[rows_own], h2z.at[rows_other])
    swap_back_low = exchange(16, h2.at[rows_own], got_low.at[rows_own])
    swap_out_low = exchange(17, h2.at[rows_other], got_low.at[rows_other])
    send_back = remote(h2.at[rows_own], pair_back, csend, crecv, 18, pair)
    send_out = remote(h2.at[rows_other], pair_out, csend, crecv, 19, pair)

    def bias_copy(k, arriving=False):
        at = bias_all.at[flip(z, k) if arriving else z]
        return remote(at, at, zsend, zrecv, k, along_z(k))

    barrier = pltpu.get_barrier_semaphore()
    peers = [partner, along_x, along_y, across, along_z(1), along_z(2), along_z(3)]
    for peer in peers:
        pl.semaphore_signal(barrier, inc=1, device_id=peer, device_id_type=MESH_ID)
    pl.semaphore_wait(barrier, len(peers))

    start_source(attn)
    bias_all[z] = jnp.zeros(bias_all.shape[1:], F32)
    part = qkv_bias_in.shape[1] // 2
    for side in range(2):

        @pl.when(r == side)
        def _():
            bias_all[z, 0:1, :half] = expand_bias_in[side * half : (side + 1) * half].reshape(1, half)
            for i in range(2):
                at = half + 2 * i * part
                bias_all[z, 0:1, at : at + part] = qkv_bias_in[i : i + 1, side * part : (side + 1) * part]

    finish_source(attn)
    start_z(attn)
    for k in (1, 2, 3):
        bias_copy(k).start()
    start_source(mlp)

    def as_row(ref):
        return ref[...].reshape(1, width)

    gain_one, shift_one, gain_two, shift_two, proj_bias, shrink_bias = (
        as_row(ref) for ref in (gain_one_in, shift_one_in, gain_two_in, shift_two_in, proj_bias_in, shrink_bias_in)
    )

    def over_rows(body):
        @pl.loop(0, own // CHUNK)
        def _(m):
            body(pl.ds(pl.multiple_of(m * CHUNK, CHUNK), CHUNK))

    def column_sum(value):
        return jnp.sum(value, axis=0, keepdims=True)

    def normalize(value):
        center = value - jnp.mean(value, axis=1, keepdims=True)
        inverse = lax.rsqrt(jnp.mean(center * center, axis=1, keepdims=True) + EPS)
        return center * inverse, inverse

    def norm_back(grad, gain, xhat, inverse):
        scaled = grad * gain
        mean = jnp.mean(scaled, axis=1, keepdims=True)
        along = jnp.mean(scaled * xhat, axis=1, keepdims=True)
        return (scaled - mean - xhat * along) * inverse

    early[...] = jnp.zeros_like(early)
    late[...] = jnp.zeros_like(late)

    def spread_rows(source, target):
        def move(stage):
            load = pltpu.make_async_copy(source, stage, local.at[8])
            load.start()
            load.wait()

            @pl.loop(0, SIDE)
            def _(i):
                both = stage[pl.ds(i * SIDE, SIDE)].astype(F32)
                for w in range(both.shape[1]):
                    some = jnp.concatenate([both[:, w], jnp.zeros((SIDE_PAD - SIDE, width), F32)], axis=0)
                    at = pl.multiple_of(w * WROWS + i * SIDE_PAD, SIDE_PAD)
                    target[pl.ds(at, SIDE_PAD)] = some.astype(BF)

        pl.run_scoped(move, pltpu.VMEM(source.shape, BF))

    spread_rows(tokens_in, tokens)
    count = mask_in.shape[0]
    mask = jnp.concatenate([mask_in[...].astype(F32), jnp.zeros((count, 2 * LANES - SIDE * SIDE), F32)], axis=1)
    mask = jnp.concatenate([mask, jnp.zeros((8 - count, 2 * LANES), F32)], axis=0).T
    keep[...] = jnp.zeros_like(keep)
    for i in range(SIDE):
        for w in range(count):
            at = w * WROWS + i * SIDE_PAD
            keep[at : at + SIDE] = mask[i * SIDE : (i + 1) * SIDE, w : w + 1]

    def first_rows(rows):
        value = tokens[rows].astype(F32)
        valid = keep[rows]
        xhat, _ = normalize(value)
        h1[rows] = ((xhat * gain_one + shift_one) * valid).astype(BF)
        early[0:1, :] += column_sum(valid * value * value)
        early[5:6, :] += jnp.broadcast_to(column_sum(valid), (1, width))

    over_rows(first_rows)
    swap_h1.start()
    spread_rows(out_grad_in, gm)
    swap_grad.start()
    rel_pad[...] = jnp.zeros_like(rel_pad)
    rel_pad[0, : rel_h_in.shape[0]] = rel_h_in[...]
    rel_pad[1, : rel_w_in.shape[0]] = rel_w_in[...]
    relative_tables(rel_pad.at[0], rel_pad.at[1], rel_query, rel_back)
    total[...] = jnp.zeros_like(total)
    swap_h1.wait_recv()

    def bias_q_of(s):
        return bias_all[s, 0:1, half : half + qkv_width]

    def bias_e_of(s):
        return bias_all[s, 0:1, :half]

    finish_source(mlp)

    def start_far():
        for a in mlp:
            gather_far(a).start()
        pair_gm.start()

    @pl.loop(0, 4)
    def _(i):
        @pl.when(i == 1)
        def _():
            relay(attn, 1)
            share(attn, 1)

            relay(attn, 2)
            share(attn, 2)

            @pl.when(is_end)
            def _():
                start_far()

            relay(attn, 3)
            pass_diagonal(attn, 1)
            share(attn, 3)
            pass_diagonal(attn, 2)

            @pl.when(is_inner)
            def _():
                start_far()

            for k in (1, 2, 3):
                bias_copy(k, True).wait_recv()

        @pl.when(i > 0)
        def _():
            finish_slab(attn, i)

        @pl.when(i == 2)
        def _():
            pass_diagonal(attn, 3)

        @pl.when(((i == 2) & is_inner) | ((i == 3) & is_end))
        def _():
            share_far(mlp)

        s = slab_of(i)

        def half_done():
            @pl.when(i == 3)
            def _():
                swap_attn.start()

        attention_slab(
            s, h1, wq, wp, bias_q_of(s), rel_query, codes, attended, total, heads, half, half_done
        )


    swap_attn.wait()

    def middle_rows(rows):
        value = tokens[rows].astype(F32)
        valid = keep[rows]
        attn_out = total[rows] + xr[rows] + proj_bias
        mid = value + attn_out
        middle[rows] = mid
        xhat, _ = normalize(mid)
        h2[rows] = (xhat * gain_two + shift_two).astype(BF)
        early[1:2, :] += column_sum(valid * mid * mid)
        early[3:4, :] += column_sum(valid * attn_out * attn_out)

    over_rows(middle_rows)
    swap_h2.start()
    pair_h2.start()
    total[...] = jnp.zeros_like(total)
    back[...] = jnp.zeros_like(back)
    bias_e[...] = jnp.zeros_like(bias_e)
    bias_q[...] = jnp.zeros_like(bias_q)
    rel_acc[...] = jnp.zeros_like(rel_acc)
    swap_grad.wait()

    def weight_grads(p, j):
        for side in range(2):
            columns = slice(side * half, side * half + half)
            for buf, left, right in (
                (we, normed[p, :, columns], gpre[...]),
                (ws, act[...], grads[p, :, columns]),
            ):
                value = dot_tn(left, right).reshape(buf.shape[2:])
                value = value + jnp.where(p > 0, buf[2 + j, side].astype(F32), 0.0)
                buf[2 + j, side] = value.astype(BF)

    def own_rows(rows):
        xr[rows] = xr[rows] + total[rows]
        xr2[rows] = xr2[rows] + back[rows]

    def other_rows(rows):
        return pl.ds(pl.multiple_of(rows.start + own, CHUNK), CHUNK)

    def back_low_rows(rows):
        h2[rows] = back[other_rows(rows)].astype(BF)

    def out_low_rows(rows):
        h2[other_rows(rows)] = total[other_rows(rows)].astype(BF)

    def back_sum_rows(rows):
        h2[rows] = (back[rows] + got_low[rows].astype(F32)).astype(BF)

    def out_sum_rows(rows):
        h2[other_rows(rows)] = (total[rows] + got_low[other_rows(rows)].astype(F32)).astype(BF)

    def between_passes():
        pair_h2.wait()
        swap_h2z.start()
        swap_mlp.wait()
        swap_gh2.wait()
        over_rows(own_rows)
        total[...] = jnp.zeros_like(total)
        back[...] = jnp.zeros_like(back)
        swap_gmz.wait()
        swap_h2z.wait()

    def start_pair_sums():
        over_rows(back_low_rows)
        swap_back_low.start()
        over_rows(out_low_rows)
        swap_out_low.start()

    def send_pair_sums():
        swap_back_low.wait()
        over_rows(back_sum_rows)
        send_back.start()
        swap_out_low.wait()
        over_rows(out_sum_rows)
        send_out.start()

    @pl.loop(0, 8)
    def _(t):
        p, j = t // 4, t // 2 % 2
        s = (1 - j) * z + j * remote_slab

        @pl.when(t == 1)
        def _():
            pass_diagonal(mlp, 1)
            swap_h2.wait()

        @pl.when(t == 2)
        def _():
            finish_slab(mlp, 1)
            pair_gm.wait_recv()
            swap_gmz.start()

        @pl.when(t == 3)
        def _():
            swap_mlp.start()
            swap_gh2.start()

        @pl.when(t == 4)
        def _():
            between_passes()

        @pl.when(t == 7)
        def _():
            start_pair_sums()

        mlp_rows(
            s, j, (t + j) % 2, normed.at[p], grads.at[p], we, ws, bias_e_of(s), act, gpre, total, back, bias_e, half
        )

        @pl.when(t == 7)
        def _():
            send_pair_sums()

        @pl.when(t % 2 == 1)
        def _():
            weight_grads(p, j)

            @pl.when(p == 1)
            def _():
                reduce_one(mlp, j)

    sent_far(mlp)
    reduce_two(mlp, 0)
    send_back.wait_recv()
    back_load = pltpu.make_async_copy(pair_back, gmz.at[rows_own], local.at[8])
    back_load.start()
    back_load.wait()

    pair_gm.wait_send()

    def middle_back_rows(rows):
        mid = middle[rows]
        grad_out = gm[rows].astype(F32)
        early[9:10, :] += column_sum(grad_out)
        grad = xr2[rows] + gmz[rows].astype(F32)
        xhat, inverse = normalize(mid)
        early[6:7, :] += column_sum(grad * xhat)
        early[7:8, :] += column_sum(grad)
        grad_mid = grad_out + norm_back(grad, gain_two, xhat, inverse)
        xr2[rows] = grad_mid
        low = grad_mid.astype(BF)
        gm[rows] = low
        early[8:9, :] += column_sum(low.astype(F32))

    over_rows(middle_back_rows)
    swap_ga.start()

    def result_rows(rows):
        valid = keep[rows]
        mlp_out = xr[rows] + gmz[other_rows(rows)].astype(F32) + shrink_bias
        result = middle[rows] + mlp_out
        h2[rows] = result.astype(BF)
        early[2:3, :] += column_sum(valid * result * result)
        early[4:5, :] += column_sum(valid * mlp_out * mlp_out)

    back[...] = jnp.zeros_like(back)
    for i in range(4):
        sent_slab(attn, i)
    reduce_two(mlp, 1)
    swap_ga.wait()

    out_load = pltpu.make_async_copy(pair_out, gmz.at[rows_other], local.at[8])
    result_store = pltpu.make_async_copy(h2.at[rows_own], block_out, local.at[8])

    def finish_result():
        send_back.wait_send()
        send_out.wait_recv()
        out_load.start()
        out_load.wait()
        over_rows(result_rows)
        result_store.start()

    stages = ((partner,), (along_z(1), along_z(2), along_z(3)), (along_x, along_y, across))
    early_sums = (((early, early_got),), 20)
    late_sums = (((late, late_got), (rel, rel_got)), 27)

    def small_copies(sums, stage):
        pairs, base = sums
        first = (0, 1, 4)[stage]
        for i, device in enumerate(stages[stage]):
            for j, (src, got) in enumerate(pairs):
                index = base + (first + i) * len(pairs) + j
                yield src, got, first + i, remote(src, got.at[first + i], csend, crecv, index, device)

    def small_start(sums, stage):
        for _, _, _, copy in small_copies(sums, stage):
            copy.start()

    def small_finish(sums, stage):
        copies = list(small_copies(sums, stage))
        for _, _, _, copy in copies:
            copy.wait()
        for src, got, place, _ in copies:
            src[...] += got[place]

    def on_side(act_on):
        for side in range(2):

            @pl.when(r == side)
            def _():
                act_on(side)

    def fill_early(side):
        for s in range(4):
            early[10 + s : 11 + s, side * half : (side + 1) * half] = bias_e[s]

    early_store = pltpu.make_async_copy(early, early_out, local.at[9])

    @pl.loop(0, 4)
    def _(n):
        s = slab_of(3 - n)
        g = slot(0, n)

        def half_done():
            @pl.when(n == 0)
            def _():
                reduce_three(mlp, 0)

            @pl.when(n == 2)
            def _():
                small_finish(early_sums, 0)
                small_start(early_sums, 1)
                reduce_four((2,))

            @pl.when(n == 3)
            def _():
                swap_gh1.start()
                small_finish(early_sums, 1)
                small_start(early_sums, 2)
                reduce_four((3,))

        attention_back_slab(
            s, h1, gm, wq, wp, bias_q_of(s), rel_query, rel_back, codes, act, back, bias_q, rel_acc, heads, half, half_done
        )

        @pl.when(n > 0)
        def _():
            reduce_two(attn, n - 1)

        for side in range(2):
            columns = slice(side * half, side * half + half)
            wq[g, side] = dot_tn(act[:, :qkv_width], h1[:, columns]).astype(BF).reshape(wq.shape[2:])
            wp[g, side] = dot_tn(attended[s], gm[:, columns]).astype(BF).reshape(wp.shape[2:])
        reduce_one(attn, n)

        @pl.when((n > 1) & is_end)
        def _():
            reduce_three(attn, n - 2)

        @pl.when((n == 3) & is_inner)
        def _():
            reduce_three(attn, 0)

        @pl.when(n == 0)
        def _():
            reduce_three(mlp, 1)

        @pl.when(n == 1)
        def _():
            finish_result()
            on_side(fill_early)
            small_start(early_sums, 0)

    swap_gh1.wait()

    def input_rows(rows):
        value = tokens[rows].astype(F32)
        grad = (back[rows] + total[other_rows(rows)]) * keep[rows]
        xhat, inverse = normalize(value)
        late[0:1, :] += column_sum(grad * xhat)
        late[1:2, :] += column_sum(grad)
        xr2[rows] = xr2[rows] + norm_back(grad, gain_one, xhat, inverse)

    over_rows(input_rows)
    input_store = pltpu.make_async_copy(xr2, input_grad, local.at[10])
    input_store.start()

    def fill_late(side):
        lanes = bias_q.shape[2]
        for s in range(4):
            late[2 + s : 3 + s, side * lanes : (side + 1) * lanes] = bias_q[s]

    on_side(fill_late)
    for part, at in ((0, 0), (1, COL_W)):
        rows = slice(at, at + 32)
        rel[part * 32 : part * 32 + 32] = rel_acc[rows] + rel_acc[LANES + at : LANES + at + 32]

    small_start(late_sums, 0)

    @pl.when(is_inner)
    def _():
        reduce_three(attn, 1)

    reduce_three(attn, 2)
    small_finish(late_sums, 0)
    small_start(late_sums, 1)
    reduce_two(attn, 3)
    reduce_five(mlp)
    reduce_three(attn, 3)
    reduce_four(attn)
    small_finish(late_sums, 1)
    small_start(late_sums, 2)
    small_finish(early_sums, 2)
    early_store.start()
    reduce_six(mlp)
    reduce_five(attn)
    small_finish(late_sums, 2)
    late_stores = [
        pltpu.make_async_copy(late, late_out, local.at[6]),
        pltpu.make_async_copy(rel, rel_out, local.at[7]),
    ]
    for copy in late_stores:
        copy.start()
    reduce_six(attn)

    swap_h1.wait_send()
    send_out.wait_send()
    for k in (1, 2, 3):
        bias_copy(k).wait_send()
    for a in range(4):
        for copy in swap_out(a) + keep_out(a):
            copy.wait()
        for kind in (1, 2, 3, 4):
            spread(a, kind).wait_send()
        for n in range(4 if a in attn else 2):
            for kind in range(4):
                reduce_copy(a, n, kind).wait_send()
            reduce_z(a, n, lambda copy: copy.wait_send())

    for copy in late_stores:
        copy.wait()
    early_store.wait()
    result_store.wait()
    input_store.wait()


def run_kernel(tokens, mask, out_grad, vectors, qkv_bias, expand_bias, rel_height, rel_width, sources):
    own, width = tokens.shape[1] * WROWS, tokens.shape[2]
    half = width // 2
    rows = [source.shape[-2] for source in sources]
    rows[0] = 3 * rows[0] // 2
    sds = jax.ShapeDtypeStruct
    any_spec = pl.BlockSpec(memory_space=pl.ANY)
    vmem_spec = pl.BlockSpec(memory_space=pltpu.VMEM)
    out_shape = [sds((own, width), BF), sds((own, width), F32)]
    out_shape += [sds(source.shape, BF) for source in sources]
    out_shape += [sds((16, width), F32), sds((8, width), F32), sds((64, LANES), F32)]
    first, second = zip(*[halves(n) for n in rows])
    out_shape += [sds((4, 2, n, half), BF) for n in first]
    out_shape += [sds((4, 2, n, half), BF) for n in second]
    out_shape += [sds((4, n, half), BF) for n in second]
    out_shape += [sds((4, n, half), BF) for n in first]
    out_shape += [sds((6, n, half), BF) for n in rows]
    out_shape += [sds((own, width), BF)] * 2
    both = 2 * own
    vmem, dma = pltpu.VMEM, pltpu.SemaphoreType.DMA
    qkv_width = 2 * rows[0]
    scratch = [vmem((count, 2, 2, n, half), BF) for count, n in zip((5, 5, 4, 4), rows)]
    scratch += [vmem((own, width), BF), vmem((own, 1), F32)]
    scratch += [vmem((both, width), BF)] + [vmem((2, both, width), BF)] * 2 + [vmem((both, width), BF)]
    scratch += [vmem((4, both, qkv_width // 3), BF)]
    scratch += [vmem((both, width), F32)] * 2
    scratch += [vmem((own, width), F32)] * 3
    scratch += [vmem((both, half), BF), vmem((both, half), BF)]
    scratch += [vmem((4, 8, width), F32), vmem((16, width), F32), vmem((7, 16, width), F32)]
    scratch += [vmem((8, width), F32), vmem((7, 8, width), F32)]
    scratch += [vmem((64, LANES), F32), vmem((7, 64, LANES), F32)]
    scratch += [vmem((4, 1, half), F32), vmem((4, 1, qkv_width), F32), vmem((2 * LANES, LANES), F32)]
    scratch += [vmem((2 * LANES, LANES), BF), vmem((3 * LANES, LANES), BF), vmem((2, 32, HEAD), F32)]
    scratch += [dma((4, 4, 6))] * 2 + [dma((4, 4, 5)), dma((4, 4, 6))] + [dma((4, 5))] * 2 + [dma((41,))] * 2
    scratch += [dma((4,))] * 2 + [dma((8,))] * 2 + [dma((11,)), dma((4,))]
    got = pl.pallas_call(
        kernel,
        out_shape=out_shape,
        in_specs=[any_spec, vmem_spec, any_spec] + [vmem_spec] * 11 + [any_spec] * 4,
        out_specs=[any_spec] * len(out_shape),
        scratch_shapes=scratch,
        compiler_params=pltpu.CompilerParams(
            collective_id=0, has_side_effects=True, vmem_limit_bytes=VMEM_LIMIT
        ),
        name="block_step",
    )(tokens, mask, out_grad, *vectors, qkv_bias, expand_bias, rel_height, rel_width, key_codes(), *sources)
    return got[:9]


def finish_kernel(early, late, rel, *refs):
    wide, (bias_q, bias_e, height, width_out, rms), rows_out = refs[:6], refs[6:11], refs[11:17]
    outs, held, full, load, store = refs[17:23], refs[23:29], refs[29:35], refs[35], refs[36]
    z = lax.axis_index("col")
    loads = [pltpu.make_async_copy(src, to, load.at[i]) for i, (src, to) in enumerate(zip(wide, held))]
    stores = [pltpu.make_async_copy(src, to, store.at[i]) for i, (src, to) in enumerate(zip(full, outs))]
    for i in (3, 2, 0, 1, 5, 4):
        loads[i].start()
    places = ((late, 0), (late, 1), (early, 6), (early, 7), (early, 8), (early, 9))
    for ref, (source, at) in zip(rows_out, places):
        ref[...] = source[at, :]
    features = early.shape[1]
    lane = lax.broadcasted_iota(jnp.int32, (1, LANES), 1)
    stats = jnp.zeros((1, LANES), F32)
    for i in range(rms.shape[0]):
        stats = jnp.where(lane == i, jnp.sum(early[i : i + 1, :], axis=1, keepdims=True), stats)
    rms[...] = jnp.sqrt(stats / (early[5:6, 0:1] * features))[0, : rms.shape[0]]
    half = features // 2
    part = bias_q.shape[1] // 2
    bias_e[...] = early[pl.ds(10 + z, 1), :].reshape(features)
    row = late[pl.ds(2 + z, 1), :]
    for side in range(2):
        for i in range(2):
            at = (3 * side + 2 * i) * part
            bias_q[i : i + 1, side * part : (side + 1) * part] = row[:, at : at + part]
    count = height.shape[0]
    turn = lax.broadcasted_iota(jnp.int32, (32, 32), 0) + lax.broadcasted_iota(jnp.int32, (32, 32), 1) == count - 1
    turned = jnp.dot(turn.astype(F32), rel[:32], precision=lax.Precision.HIGHEST, preferred_element_type=F32)
    height[...] = turned[:count, :HEAD]
    width_out[...] = rel[32 : 32 + count, :HEAD]
    for i in (3, 2, 0, 1):
        loads[i].wait()
        step = held[i].shape[0] // 5

        @pl.loop(0, 5)
        def _(m):
            at = pl.ds(pl.multiple_of(m * step, step), step)
            full[i][at] = held[i][at].astype(F32)

        stores[i].start()
    loads[5].wait()

    @pl.loop(0, SIDE)
    def _(i):
        for w in range(2):
            at = pl.multiple_of(w * WROWS + i * SIDE_PAD, SIDE_PAD)
            full[5][pl.ds(i * SIDE, SIDE), w, :] = held[5][pl.ds(at, SIDE_PAD)][:SIDE]

    stores[5].start()
    loads[4].wait()

    @pl.loop(0, SIDE)
    def _(i):
        places = [pl.multiple_of(w * WROWS + i * SIDE_PAD, SIDE_PAD) for w in range(2)]
        some = [held[4][pl.ds(at, SIDE_PAD)][:SIDE].astype(F32) for at in places]
        full[4][pl.ds(i * SIDE, SIDE)] = jnp.stack(some, axis=1).astype(BF)

    stores[4].start()
    for copy in stores:
        copy.wait()


def finish_outputs(got, part):
    early, late, rel = got[6:9]
    grads = [value.reshape(-1, value.shape[-1]) for value in got[2:6]]
    width = early.shape[1]
    sds = jax.ShapeDtypeStruct
    any_spec = pl.BlockSpec(memory_space=pl.ANY)
    vmem_spec = pl.BlockSpec(memory_space=pltpu.VMEM)
    windows = got[0].shape[0] // WROWS
    out_shape = [sds((2, 2 * part), F32), sds((width,), F32), sds((2 * SIDE - 1, HEAD), F32)]
    out_shape += [sds((2 * SIDE - 1, HEAD), F32), sds((5,), F32)] + [sds((width,), F32)] * 6
    held = grads + list(got[:2])
    final = [sds(value.shape, F32) for value in grads]
    final += [sds((SIDE * SIDE, windows, width), value.dtype) for value in got[:2]]
    out_shape += final
    return pl.pallas_call(
        finish_kernel,
        out_shape=out_shape,
        in_specs=[vmem_spec] * 3 + [any_spec] * 6,
        out_specs=[vmem_spec] * 11 + [any_spec] * 6,
        scratch_shapes=[pltpu.VMEM(value.shape, value.dtype) for value in held + final]
        + [pltpu.SemaphoreType.DMA((6,))] * 2,
        compiler_params=pltpu.CompilerParams(vmem_limit_bytes=VMEM_LIMIT),
        name="finish",
    )(early, late, rel, *held)


VMEM_LIMIT = 64 * 1024 * 1024 - 512 * 1024


def over_chips(
    tokens, valid_mask, out_grad, first_gain, first_shift, qkv_weight, qkv_bias, rel_height, rel_width,
    proj_weight, proj_bias, second_gain, second_shift, expand_weight, expand_bias, shrink_weight, shrink_bias,
):
    def turned(value):
        return value.transpose(1, 0, 2)

    rows, _, local_width = qkv_weight.shape
    part = local_width // 2
    hidden = expand_weight.shape[1] // 2
    qkv_src = qkv_weight.transpose(1, 2, 0).reshape(3, 2, part, rows)
    proj_src = proj_weight.reshape(2, 2, part // 2, proj_weight.shape[1])
    expand_src = expand_weight.reshape(2, rows // 2, 2 * hidden)
    shrink_src = shrink_weight.reshape(2, 2, hidden // 2, shrink_weight.shape[1])
    vectors = (first_gain, first_shift, second_gain, second_shift, proj_bias, shrink_bias)
    got = run_kernel(
        turned(tokens), valid_mask, turned(out_grad), vectors, qkv_bias, expand_bias, rel_height, rel_width,
        (qkv_src, proj_src, expand_src, shrink_src),
    )
    outs = finish_outputs(got, part)
    qkv_bias_sum, expand_bias_sum, height_sum, width_sum, rms = outs[:5]
    gain_one, shift_one, gain_two, shift_two, proj_bias_sum, shrink_bias_sum = outs[5:11]
    qkv_sum, proj_sum, expand_sum, shrink_sum, block_out, input_grad = outs[11:]
    return (
        turned(block_out),
        turned(input_grad),
        gain_one,
        shift_one,
        qkv_sum.reshape(3, local_width, rows).transpose(2, 0, 1),
        qkv_bias_sum,
        height_sum,
        width_sum,
        proj_sum.reshape(proj_weight.shape),
        proj_bias_sum,
        gain_two,
        shift_two,
        expand_sum.reshape(expand_weight.shape),
        expand_bias_sum,
        shrink_sum.reshape(shrink_weight.shape),
        shrink_bias_sum,
        rms,
    )


epsilon = 1e-06
highest = lax.Precision.HIGHEST


def layer_norm(values, norm_gain, norm_shift):
    center = values - jnp.mean(values, axis=-1, keepdims=True)
    spread = jnp.mean(center * center, axis=-1, keepdims=True)
    return center * lax.rsqrt(spread + epsilon) * norm_gain + norm_shift


def offset_table(span_size):
    positions = jnp.arange(span_size)
    offset = positions[:, None] - positions[None, :] + span_size - 1
    return (offset[:, :, None] == jnp.arange(2 * span_size - 1)[None, None, :]).astype(jnp.float32)


def attention_scores(
    query_rows, key_rows, rel_rows_table, rel_cols_table, onehot_table, span_size, scaling
):
    window_count, tokens_per, head_count, head_size = query_rows.shape
    rel_count = 2 * span_size - 1
    direct = (
        jnp.einsum("bthc,buhc->bhtu", query_rows, key_rows, preferred_element_type=jnp.float32)
        * scaling
    )
    query_float = query_rows.astype(jnp.float32)
    along_rows = jnp.einsum("bthc,jc->bhtj", query_float, rel_rows_table, precision=highest)
    along_cols = jnp.einsum("bthc,jc->bhtj", query_float, rel_cols_table, precision=highest)
    grid_rows = along_rows.reshape(window_count, head_count, span_size, span_size, rel_count)
    grid_cols = along_cols.reshape(window_count, head_count, span_size, span_size, rel_count)
    rel_rows = jnp.einsum("bhxyj,xkj->bhxyk", grid_rows, onehot_table, precision=highest)
    rel_cols = jnp.einsum("bhxyj,ywj->bhxyw", grid_cols, onehot_table, precision=highest)
    score_sum = direct.reshape(window_count, head_count, span_size, span_size, span_size, span_size)
    score_sum = score_sum + rel_rows[:, :, :, :, :, None] + rel_cols[:, :, :, :, None, :]
    return score_sum.reshape(window_count, head_count, tokens_per, tokens_per)


def relative_back(score_float, onehot_table, span_size):
    window_count, head_count, tokens_per, other_tokens = score_float.shape
    grid = score_float.reshape(window_count, head_count, span_size, span_size, span_size, span_size)
    rows_part = jnp.einsum("bhxykw,xkj->bhxyj", grid, onehot_table, precision=highest)
    cols_part = jnp.einsum("bhxykw,ywj->bhxyj", grid, onehot_table, precision=highest)
    return (
        rows_part.reshape(window_count, head_count, tokens_per, -1),
        cols_part.reshape(window_count, head_count, tokens_per, -1),
    )


def gather_weights(qkv_weight, proj_weight, expand_weight, shrink_weight):
    return (
        lax.all_gather(qkv_weight, "row", axis=0, tiled=True),
        lax.all_gather(proj_weight, "row", axis=1, tiled=True),
        lax.all_gather(expand_weight, "row", axis=0, tiled=True),
        lax.all_gather(shrink_weight, "row", axis=1, tiled=True),
    )


def gather_tokens(normed):
    return lax.all_gather(normed, "col", axis=0, tiled=True)


def gather_grads(grad_low):
    return lax.all_gather(grad_low, "col", axis=0, tiled=True)


def sum_branch(inputs_low, weight_full, own_windows):

    def term(first_row, row_count):
        return jnp.einsum(
            "btk,kd->btd", inputs_low, weight_full, preferred_element_type=jnp.float32
        )

    return lax.psum_scatter(
        term(jnp.int32(0), own_windows * lax.axis_size("col")),
        "col",
        scatter_dimension=0,
        tiled=True,
    )


def sum_input(grads_low, weight_full, own_windows):

    def term(first_row, row_count):
        return jnp.einsum("btk,dk->btd", grads_low, weight_full, preferred_element_type=jnp.float32)

    return lax.psum_scatter(
        term(jnp.int32(0), own_windows * lax.axis_size("col")),
        "col",
        scatter_dimension=0,
        tiled=True,
    )


def activate(values):
    return jax.nn.gelu(values, approximate=False)


def per_device(
    tokens,
    valid_mask,
    out_grad,
    first_gain,
    first_shift,
    qkv_weight,
    qkv_bias,
    rel_height,
    rel_width,
    proj_weight,
    proj_bias,
    second_gain,
    second_shift,
    expand_weight,
    expand_bias,
    shrink_weight,
    shrink_bias,
):
    span_size = (rel_height.shape[0] + 1) // 2
    head_size = rel_height.shape[1]
    local_width = qkv_weight.shape[2]
    head_count = local_width // head_size
    own_windows = tokens.shape[0]
    tokens_per = tokens.shape[1]
    model_width = tokens.shape[2]
    scaling = head_size ** (-0.5)
    onehot_table = offset_table(span_size)
    inputs = tokens.astype(jnp.float32)
    keep_mask = valid_mask.astype(jnp.float32)[:, :, None]

    def first_norm(values, norm_gain, norm_shift):
        return layer_norm(values, norm_gain, norm_shift) * keep_mask

    qkv_full, proj_full, expand_full, shrink_full = gather_weights(
        qkv_weight, proj_weight, expand_weight, shrink_weight
    )
    normed_first, first_back = jax.vjp(first_norm, inputs, first_gain, first_shift)
    first_all = gather_tokens(normed_first.astype(jnp.bfloat16))
    all_windows = first_all.shape[0]
    bias_rows = jnp.stack([qkv_bias[0], jnp.zeros_like(qkv_bias[0]), qkv_bias[1]])
    projected = (
        jnp.einsum("btd,dsk->btsk", first_all, qkv_full, preferred_element_type=jnp.float32)
        + bias_rows
    )
    projected = projected.astype(jnp.bfloat16)
    head_shape = (all_windows, tokens_per, head_count, head_size)
    query_low = projected[:, :, 0].reshape(head_shape)
    key_low = projected[:, :, 1].reshape(head_shape)
    value_low = projected[:, :, 2].reshape(head_shape)
    scores = attention_scores(
        query_low, key_low, rel_height, rel_width, onehot_table, span_size, scaling
    )
    top_score = jnp.max(scores, axis=-1, keepdims=True)
    log_total = top_score + jnp.log(jnp.sum(jnp.exp(scores - top_score), axis=-1, keepdims=True))
    probs_low = jnp.exp(scores - log_total).astype(jnp.bfloat16)
    attended = jnp.einsum(
        "bhtu,buhc->bthc", probs_low, value_low, preferred_element_type=jnp.float32
    )
    attended_low = attended.reshape(all_windows, tokens_per, local_width).astype(jnp.bfloat16)
    attn_out = sum_branch(attended_low, proj_full, own_windows) + proj_bias
    middle = inputs + attn_out
    normed_second, second_back = jax.vjp(layer_norm, middle, second_gain, second_shift)
    second_all = gather_tokens(normed_second.astype(jnp.bfloat16))
    hidden_pre = (
        jnp.einsum("btd,df->btf", second_all, expand_full, preferred_element_type=jnp.float32)
        + expand_bias
    )
    active_value, active_back = jax.vjp(activate, hidden_pre)
    hidden_low = active_value.astype(jnp.bfloat16)
    mlp_out = sum_branch(hidden_low, shrink_full, own_windows) + shrink_bias
    result = middle + mlp_out
    stat_terms = jnp.stack(
        [
            jnp.sum(keep_mask * inputs * inputs),
            jnp.sum(keep_mask * middle * middle),
            jnp.sum(keep_mask * result * result),
            jnp.sum(keep_mask * attn_out * attn_out),
            jnp.sum(keep_mask * mlp_out * mlp_out),
        ]
    )
    valid_count = jnp.sum(keep_mask)
    stat_total, count_total = lax.psum((stat_terms, valid_count), ("dp", "row", "col"))
    out_float = out_grad.astype(jnp.float32)
    qkv_full, proj_full, expand_full, shrink_full = gather_weights(
        qkv_weight, proj_weight, expand_weight, shrink_weight
    )
    mlp_grad_low = out_float.astype(jnp.bfloat16)
    shrink_bias_grad = jnp.sum(mlp_grad_low, axis=(0, 1), dtype=jnp.float32)
    mlp_grad_all = gather_grads(mlp_grad_low)
    shrink_grad_full = jnp.einsum(
        "btf,btd->fd", hidden_low, mlp_grad_all, preferred_element_type=jnp.float32
    )
    hidden_grad = jnp.einsum(
        "btd,fd->btf", mlp_grad_all, shrink_full, preferred_element_type=jnp.float32
    )
    pre_grad_low = active_back(hidden_grad)[0].astype(jnp.bfloat16)
    expand_bias_grad = jnp.sum(pre_grad_low, axis=(0, 1), dtype=jnp.float32)
    expand_grad_full = jnp.einsum(
        "btd,btf->df", second_all, pre_grad_low, preferred_element_type=jnp.float32
    )
    second_grad = sum_input(pre_grad_low, expand_full, own_windows)
    middle_part, second_gain_grad, second_shift_grad = second_back(second_grad)
    middle_grad = out_float + middle_part
    attn_grad_low = middle_grad.astype(jnp.bfloat16)
    proj_bias_grad = jnp.sum(attn_grad_low, axis=(0, 1), dtype=jnp.float32)
    attn_grad_all = gather_grads(attn_grad_low)
    proj_grad_full = jnp.einsum(
        "btk,btd->kd", attended_low, attn_grad_all, preferred_element_type=jnp.float32
    )
    attended_grad = jnp.einsum(
        "btd,kd->btk", attn_grad_all, proj_full, preferred_element_type=jnp.float32
    )
    attended_grad = attended_grad.astype(jnp.bfloat16).reshape(head_shape)
    scores_again = attention_scores(
        query_low, key_low, rel_height, rel_width, onehot_table, span_size, scaling
    )
    probs_float = jnp.exp(scores_again - log_total)
    probs_again = probs_float.astype(jnp.bfloat16)
    prob_grad = jnp.einsum(
        "bthc,buhc->bhtu", attended_grad, value_low, preferred_element_type=jnp.float32
    )
    value_grad = jnp.einsum(
        "bhtu,bthc->buhc", probs_again, attended_grad, preferred_element_type=jnp.float32
    )
    score_grad = probs_float * (
        prob_grad - jnp.sum(probs_float * prob_grad, axis=-1, keepdims=True)
    )
    score_low = score_grad.astype(jnp.bfloat16)
    rows_grad, cols_grad = relative_back(score_low.astype(jnp.float32), onehot_table, span_size)
    query_float = query_low.astype(jnp.float32)
    query_grad = (
        jnp.einsum("bhtu,buhc->bthc", score_low, key_low, preferred_element_type=jnp.float32)
        * scaling
    )
    query_grad = query_grad + jnp.einsum("bhtj,jc->bthc", rows_grad, rel_height, precision=highest)
    query_grad = query_grad + jnp.einsum("bhtj,jc->bthc", cols_grad, rel_width, precision=highest)
    key_grad = (
        jnp.einsum("bhtu,bthc->buhc", score_low, query_low, preferred_element_type=jnp.float32)
        * scaling
    )
    rel_height_grad = jnp.einsum("bhtj,bthc->jc", rows_grad, query_float, precision=highest)
    rel_width_grad = jnp.einsum("bhtj,bthc->jc", cols_grad, query_float, precision=highest)
    flat_shape = (all_windows, tokens_per, local_width)
    qkv_grad_low = jnp.stack(
        [
            query_grad.reshape(flat_shape),
            key_grad.reshape(flat_shape),
            value_grad.reshape(flat_shape),
        ],
        axis=2,
    ).astype(jnp.bfloat16)
    qkv_bias_grad = jnp.sum(qkv_grad_low[:, :, 0::2], axis=(0, 1), dtype=jnp.float32)
    qkv_grad_full = jnp.einsum(
        "btd,btsk->dsk", first_all, qkv_grad_low, preferred_element_type=jnp.float32
    )
    first_grad = sum_input(
        qkv_grad_low.reshape(all_windows, tokens_per, 3 * local_width),
        qkv_full.reshape(qkv_full.shape[0], 3 * local_width),
        own_windows,
    )
    input_part, first_gain_grad, first_shift_grad = first_back(first_grad)
    input_grad = middle_grad + input_part
    qkv_rows, proj_rows, expand_rows, shrink_rows = (
        lax.psum_scatter(qkv_grad_full, "row", scatter_dimension=0, tiled=True),
        lax.psum_scatter(proj_grad_full, "row", scatter_dimension=1, tiled=True),
        lax.psum_scatter(expand_grad_full, "row", scatter_dimension=0, tiled=True),
        lax.psum_scatter(shrink_grad_full, "row", scatter_dimension=1, tiled=True),
    )
    qkv_sum, proj_sum, expand_sum, shrink_sum = lax.psum(
        (qkv_rows, proj_rows, expand_rows, shrink_rows), "dp"
    )
    qkv_bias_sum, expand_bias_sum = lax.psum((qkv_bias_grad, expand_bias_grad), ("dp", "row"))
    (
        gain_one_sum,
        shift_one_sum,
        gain_two_sum,
        shift_two_sum,
        proj_bias_sum,
        shrink_bias_sum,
        height_sum,
        width_sum,
    ) = lax.psum(
        (
            first_gain_grad,
            first_shift_grad,
            second_gain_grad,
            second_shift_grad,
            proj_bias_grad,
            shrink_bias_grad,
            rel_height_grad,
            rel_width_grad,
        ),
        ("dp", "row", "col"),
    )
    rms = jnp.sqrt(stat_total / (count_total * model_width))
    return (
        result.astype(jnp.bfloat16),
        input_grad,
        gain_one_sum,
        shift_one_sum,
        qkv_sum,
        qkv_bias_sum,
        height_sum,
        width_sum,
        proj_sum,
        proj_bias_sum,
        gain_two_sum,
        shift_two_sum,
        expand_sum,
        expand_bias_sum,
        shrink_sum,
        shrink_bias_sum,
        rms,
    )


def choose(mesh):
    fits = tuple(mesh.shape[name] for name in ("dp", "row", "col")) == (4, 2, 4)
    return over_chips if fits else per_device


def solution(mesh):
    in_specs = (
        P(("dp", "row", "col"), None, None),
        P(("dp", "row", "col"), None),
        P(("dp", "row", "col"), None, None),
        P(),
        P(),
        P("row", None, "col"),
        P(None, "col"),
        P(),
        P(),
        P("col", "row"),
        P(),
        P(),
        P(),
        P("row", "col"),
        P("col"),
        P("col", "row"),
        P(),
    )
    out_specs = (
        P(("dp", "row", "col"), None, None),
        P(("dp", "row", "col"), None, None),
        P(),
        P(),
        P("row", None, "col"),
        P(None, "col"),
        P(),
        P(),
        P("col", "row"),
        P(),
        P(),
        P(),
        P("row", "col"),
        P("col"),
        P("col", "row"),
        P(),
        P(),
    )
    return jax.shard_map(
        choose(mesh), mesh=mesh, in_specs=in_specs, out_specs=out_specs, check_vma=False
    )
```

profile of v0, /device:TPU:0, one launch (start us, length us, event | category | flops | bytes accessed | tf_op | source)
XLA Modules:
  0.0 315.2 jit_solution(1184536079835203203)
XLA Ops:
  0.7 304.7 %block_step.1 = (bf16[448,1280]{1,0:T(8,128)(2,1)}, f32[448,1280]{1,0:T(8,128)}, bf16[3,2,160,640]{3,2,1,0:T(8,128)(2,1)}, bf16[2,2,80,640]{3,2,1,0:T(8,128)(2,1...) custom-call(bf16[196,2,1280]{2,1,0:T(2,128)(2,1)} %bitcast.23, ...), custom_call_target="tpu_custom_call" | custom-call | tf_op jit(solution)/shard_map/block_step/pallas_call | solution.py:1189
  305.4 9.7 %finish.1 = (f32[2,320]{1,0:T(2,128)}, f32[1280]{0:T(1024)}, f32[27,80]{1,0:T(8,128)}, f32[27,80]{1,0:T(8,128)}, f32[5]{0:T(128)}, /*index=5*/f32[1280]{0:T(1024...) custom-call(f32[16,1280]{1,0:T(8,128)} %get-tuple-element.43.early, ...), custom_call_target="tpu_custom_call" | custom-call | tf_op jit(solution)/shard_map/finish/pallas_call | solution.py:1279
where the time goes:
time: 319 us; the launch traced here: 315 us
  Pallas kernels  314 us (98%)
    pallas_call x1, Pallas kernels, run_kernel(): pl.pallas_call(kernel, out_shape=out_shape, in_specs=[any_spec, vmem_spec...  305 us
    pallas_call x1, Pallas kernels, finish_outputs(): pl.pallas_call(finish_kernel, out_shape=out_shape, in_specs=[vmem_spec] *...  9.72 us

commit v1 on v0

--- a/solution.py
+++ b/solution.py
@@ -184,13 +184,18 @@
 PDF_SCALE = 0.3989422804014327
 
 
+def both_blocks(ref, slab):
+    value = ref[slab]
+    return value.reshape(4 * value.shape[2], value.shape[3])
+
+
 def mlp_rows(s, place, m, h2, gm, we, ws, bias, act, gpre, total, back, bias_grad, half):
     count = h2.shape[0] // 2
 
     @pl.loop(0, 1)
     def _(step):
         rows = pl.ds(pl.multiple_of((m + step) * count, count), count)
-        pre = dot(h2[rows, :half], block(we, place, 0)) + dot(h2[rows, half:], block(we, place, 1)) + bias
+        pre = dot(h2[rows, :], both_blocks(we, place)) + bias
         cdf = 0.5 + 0.5 * lax.erf(pre * SQRT_HALF)
         slope = cdf + pre * (PDF_SCALE * jnp.exp(-0.5 * pre * pre))
         act_low = (pre * cdf).astype(BF)
@@ -201,8 +206,7 @@
         bias_grad[s] += jnp.sum(gpre_low.astype(F32), axis=0, keepdims=True)
         total[rows, :half] += dot(act_low, block(ws, place, 0))
         total[rows, half:] += dot(act_low, block(ws, place, 1))
-        back[rows, :half] += dot_nt(gpre_low, block(we, place, 0))
-        back[rows, half:] += dot_nt(gpre_low, block(we, place, 1))
+        back[rows, :] += dot_nt(gpre_low, both_blocks(we, place))
 
 
 def attention_back_slab(
@@ -767,14 +771,10 @@
     def _(i):
         @pl.when(i == 1)
         def _():
-            relay(attn, 1)
-            share(attn, 1)
-
-            relay(attn, 2)
-            share(attn, 2)
-
             @pl.when(is_end)
             def _():
+                relay(attn, 2)
+                share(attn, 2)
                 start_far()
 
             relay(attn, 3)
@@ -804,6 +804,16 @@
         s = slab_of(i)
 
         def half_done():
+            @pl.when(i == 0)
+            def _():
+                relay(attn, 1)
+                share(attn, 1)
+
+                @pl.when(is_inner)
+                def _():
+                    relay(attn, 2)
+                    share(attn, 2)
+
             @pl.when(i == 3)
             def _():
                 swap_attn.start()
@@ -836,16 +846,18 @@
     rel_acc[...] = jnp.zeros_like(rel_acc)
     swap_grad.wait()
 
-    def weight_grads(p, j):
-        for side in range(2):
-            columns = slice(side * half, side * half + half)
-            for buf, left, right in (
-                (we, normed[p, :, columns], gpre[...]),
-                (ws, act[...], grads[p, :, columns]),
-            ):
-                value = dot_tn(left, right).reshape(buf.shape[2:])
-                value = value + jnp.where(p > 0, buf[2 + j, side].astype(F32), 0.0)
-                buf[2 + j, side] = value.astype(BF)
+    def add_grad(buf, p, j, side, value):
+        value = value.reshape(buf.shape[2:]) + jnp.where(p > 0, buf[2 + j, side].astype(F32), 0.0)
+        buf[2 + j, side] = value.astype(BF)
+
+    def weight_grads(p, j, done):
+        sides = [(side, slice(side * half, side * half + half)) for side in range(2)]
+        for side, columns in sides:
+            add_grad(we, p, j, side, dot_tn(normed[p, :, columns], gpre[...]))
+        done((2,))
+        for side, columns in sides:
+            add_grad(ws, p, j, side, dot_tn(act[...], grads[p, :, columns]))
+        done((3,))
 
     def own_rows(rows):
         xr[rows] = xr[rows] + total[rows]
@@ -893,7 +905,7 @@
 
     @pl.loop(0, 8)
     def _(t):
-        p, j = t // 4, t // 2 % 2
+        p, j = t // 4, (t // 2 + t // 4) % 2
         s = (1 - j) * z + j * remote_slab
 
         @pl.when(t == 1)
@@ -921,7 +933,7 @@
             start_pair_sums()
 
         mlp_rows(
-            s, j, (t + j) % 2, normed.at[p], grads.at[p], we, ws, bias_e_of(s), act, gpre, total, back, bias_e, half
+            s, j, (t + t // 2) % 2, normed.at[p], grads.at[p], we, ws, bias_e_of(s), act, gpre, total, back, bias_e, half
         )
 
         @pl.when(t == 7)
@@ -930,14 +942,16 @@
 
         @pl.when(t % 2 == 1)
         def _():
-            weight_grads(p, j)
-
-            @pl.when(p == 1)
-            def _():
-                reduce_one(mlp, j)
+            def done(group):
+                @pl.when(t == 5)
+                def _():
+                    reduce_one(group, 1)
+
+            weight_grads(p, j, done)
 
     sent_far(mlp)
-    reduce_two(mlp, 0)
+    reduce_two(mlp, 1)
+    reduce_one(mlp, 0)
     send_back.wait_recv()
     back_load = pltpu.make_async_copy(pair_back, gmz.at[rows_own], local.at[8])
     back_load.start()
@@ -973,7 +987,7 @@
     back[...] = jnp.zeros_like(back)
     for i in range(4):
         sent_slab(attn, i)
-    reduce_two(mlp, 1)
+    reduce_three(mlp, 1)
     swap_ga.wait()
 
     out_load = pltpu.make_async_copy(pair_out, gmz.at[rows_other], local.at[8])
@@ -1031,20 +1045,21 @@
         def half_done():
             @pl.when(n == 0)
             def _():
-                reduce_three(mlp, 0)
+                reduce_two(mlp, 0)
+
+            @pl.when(n == 1)
+            def _():
+                reduce_four((2,))
 
             @pl.when(n == 2)
             def _():
                 small_finish(early_sums, 0)
                 small_start(early_sums, 1)
-                reduce_four((2,))
+                reduce_four((3,))
 
             @pl.when(n == 3)
             def _():
                 swap_gh1.start()
-                small_finish(early_sums, 1)
-                small_start(early_sums, 2)
-                reduce_four((3,))
 
         attention_back_slab(
             s, h1, gm, wq, wp, bias_q_of(s), rel_query, rel_back, codes, act, back, bias_q, rel_acc, heads, half, half_done
@@ -1070,7 +1085,7 @@
 
         @pl.when(n == 0)
         def _():
-            reduce_three(mlp, 1)
+            reduce_three(mlp, 0)
 
         @pl.when(n == 1)
         def _():
@@ -1108,18 +1123,21 @@
     def _():
         reduce_three(attn, 1)
 
-    reduce_three(attn, 2)
     small_finish(late_sums, 0)
     small_start(late_sums, 1)
+    reduce_three(attn, 2)
+    reduce_five((2,))
     reduce_two(attn, 3)
-    reduce_five(mlp)
+    reduce_five((3,))
+    small_finish(early_sums, 1)
+    small_start(early_sums, 2)
     reduce_three(attn, 3)
     reduce_four(attn)
     small_finish(late_sums, 1)
     small_start(late_sums, 2)
+    reduce_six(mlp)
     small_finish(early_sums, 2)
     early_store.start()
-    reduce_six(mlp)
     reduce_five(attn)
     small_finish(late_sums, 2)
     late_stores = [

time: 319 us -> 305 us (0.956)
  Pallas kernels: 314 us -> 302 us
    pallas_call x1, Pallas kernels: 305 us -> 292 us  [run_kernel(): pl.pallas_call(kernel, out_shape=out_shape, in_specs=[any_spec, vmem_spec...]
where the time goes in v1:
time: 305 us; the launch traced here: 302 us
  Pallas kernels  302 us (99%)
    pallas_call x1, Pallas kernels, run_kernel(): pl.pallas_call(kernel, out_shape=out_shape, in_specs=[any_spec, vmem_spec...  292 us
    pallas_call x1, Pallas kernels, finish_outputs(): pl.pallas_call(finish_kernel, out_shape=out_shape, in_specs=[vmem_spec] *...  9.72 us

profile of v1, /device:TPU:0, one launch (start us, length us, event | category | flops | bytes accessed | tf_op | source)
XLA Modules:
  0.0 302.4 jit_solution(9246224806804815204)
XLA Ops:
  0.7 291.8 %block_step.1 = (bf16[448,1280]{1,0:T(8,128)(2,1)}, f32[448,1280]{1,0:T(8,128)}, bf16[3,2,160,640]{3,2,1,0:T(8,128)(2,1)}, bf16[2,2,80,640]{3,2,1,0:T(8,128)(2,1...) custom-call(bf16[196,2,1280]{2,1,0:T(2,128)(2,1)} %bitcast.23, ...), custom_call_target="tpu_custom_call" | custom-call | tf_op jit(solution)/shard_map/block_step/pallas_call | solution.py:1207
  292.5 9.7 %finish.1 = (f32[2,320]{1,0:T(2,128)}, f32[1280]{0:T(1024)}, f32[27,80]{1,0:T(8,128)}, f32[27,80]{1,0:T(8,128)}, f32[5]{0:T(128)}, /*index=5*/f32[1280]{0:T(1024...) custom-call(f32[16,1280]{1,0:T(8,128)} %get-tuple-element.43.early, ...), custom_call_target="tpu_custom_call" | custom-call | tf_op jit(solution)/shard_map/finish/pallas_call | solution.py:1297

commit v2 on v1

--- a/solution.py
+++ b/solution.py
@@ -270,7 +270,7 @@
     block_out, input_grad, qkv_out, proj_out, expand_out, shrink_out, early_out, late_out, rel_out,
     rxq, rxp, rxe, rxs, ryq, ryp, rye, rys, rx2q, rx2p, rx2e, rx2s, ry2q, ry2p, ry2e, ry2s, rzq, rzp, rze, rzs, pair_back, pair_out,
     wq, wp, we, ws, tokens, keep, h1, grads, normed, got_low, attended, total, back, xr, xr2, middle, act, gpre,
-    bias_all, early, early_got, late, late_got, rel, rel_got, bias_e, bias_q, rel_acc, rel_query, rel_back, rel_pad,
+    bias_all, early, early_full, early_half, late, late_full, late_half, rel, rel_full, rel_half, bias_e, bias_q, rel_acc, rel_query, rel_back, rel_pad,
     gsend, grecv, rsend, rrecv, fsend, frecv, csend, crecv, zsend, zrecv, qsend, qrecv, local, qlocal,
 ):
     d, r, z = lax.axis_index("dp"), lax.axis_index("row"), lax.axis_index("col")
@@ -991,7 +991,20 @@
     swap_ga.wait()
 
     out_load = pltpu.make_async_copy(pair_out, gmz.at[rows_other], local.at[8])
-    result_store = pltpu.make_async_copy(h2.at[rows_own], block_out, local.at[8])
+
+    def interleave(source, target):
+        def move(stage):
+            @pl.loop(0, SIDE)
+            def _(i):
+                places = [pl.multiple_of(w * WROWS + i * SIDE_PAD, SIDE_PAD) for w in range(stage.shape[1])]
+                some = [source[pl.ds(at, SIDE_PAD)][:SIDE].astype(F32) for at in places]
+                stage[pl.ds(i * SIDE, SIDE)] = jnp.stack(some, axis=1).astype(stage.dtype)
+
+            store = pltpu.make_async_copy(stage, target, local.at[8])
+            store.start()
+            store.wait()
+
+        pl.run_scoped(move, pltpu.VMEM(target.shape, target.dtype))
 
     def finish_result():
         send_back.wait_send()
@@ -999,19 +1012,24 @@
         out_load.start()
         out_load.wait()
         over_rows(result_rows)
-        result_store.start()
-
-    stages = ((partner,), (along_z(1), along_z(2), along_z(3)), (along_x, along_y, across))
-    early_sums = (((early, early_got),), 20)
-    late_sums = (((late, late_got), (rel, rel_got)), 27)
+
+    stages = (partner,), (along_z(1), along_z(2), along_z(3)), (along_x, along_y, across), (partner,)
+    early_sums = (((early, early_full, early_half),), 20)
+    late_sums = (((late, late_full, late_half), (rel, rel_full, rel_half)), 28)
 
     def small_copies(sums, stage):
         pairs, base = sums
-        first = (0, 1, 4)[stage]
+        first = (0, 1, 4, 7)[stage]
         for i, device in enumerate(stages[stage]):
-            for j, (src, got) in enumerate(pairs):
-                index = base + (first + i) * len(pairs) + j
-                yield src, got, first + i, remote(src, got.at[first + i], csend, crecv, index, device)
+            for q, (src, full, part) in enumerate(pairs):
+                rows = part.shape[1]
+                mine = pl.ds(pl.multiple_of(r * rows, rows), rows)
+                index = base + (first + i) * len(pairs) + q
+                if stage == 0:
+                    yield src, full, slice(None), remote(src, full, csend, crecv, index, device)
+                else:
+                    got = part.at[first + i - 1]
+                    yield src, got, mine, remote(src.at[mine], got, csend, crecv, index, device)
 
     def small_start(sums, stage):
         for _, _, _, copy in small_copies(sums, stage):
@@ -1021,8 +1039,12 @@
         copies = list(small_copies(sums, stage))
         for _, _, _, copy in copies:
             copy.wait()
-        for src, got, place, _ in copies:
-            src[...] += got[place]
+        for src, got, rows, _ in copies:
+            if stage == 3:
+                count = got.shape[0]
+                src[pl.ds(pl.multiple_of((1 - r) * count, count), count)] = got[...]
+            else:
+                src[rows] += got[...]
 
     def on_side(act_on):
         for side in range(2):
@@ -1099,18 +1121,16 @@
         value = tokens[rows].astype(F32)
         grad = (back[rows] + total[other_rows(rows)]) * keep[rows]
         xhat, inverse = normalize(value)
-        late[0:1, :] += column_sum(grad * xhat)
-        late[1:2, :] += column_sum(grad)
+        for place, value in ((8, column_sum(grad * xhat)), (10, column_sum(grad))):
+            late[place : place + 1, :] += value[:, :half]
+            late[place + 1 : place + 2, :] += value[:, half:]
         xr2[rows] = xr2[rows] + norm_back(grad, gain_one, xhat, inverse)
 
     over_rows(input_rows)
-    input_store = pltpu.make_async_copy(xr2, input_grad, local.at[10])
-    input_store.start()
 
     def fill_late(side):
-        lanes = bias_q.shape[2]
         for s in range(4):
-            late[2 + s : 3 + s, side * lanes : (side + 1) * lanes] = bias_q[s]
+            late[2 * s + side : 2 * s + side + 1, :qkv_width] = bias_q[s]
 
     on_side(fill_late)
     for part, at in ((0, 0), (1, COL_W)):
@@ -1129,6 +1149,8 @@
     reduce_five((2,))
     reduce_two(attn, 3)
     reduce_five((3,))
+    interleave(xr2, input_grad)
+    interleave(h2, block_out)
     small_finish(early_sums, 1)
     small_start(early_sums, 2)
     reduce_three(attn, 3)
@@ -1137,9 +1159,13 @@
     small_start(late_sums, 2)
     reduce_six(mlp)
     small_finish(early_sums, 2)
-    early_store.start()
+    small_start(early_sums, 3)
     reduce_five(attn)
     small_finish(late_sums, 2)
+    small_start(late_sums, 3)
+    small_finish(early_sums, 3)
+    early_store.start()
+    small_finish(late_sums, 3)
     late_stores = [
         pltpu.make_async_copy(late, late_out, local.at[6]),
         pltpu.make_async_copy(rel, rel_out, local.at[7]),
@@ -1165,8 +1191,6 @@
     for copy in late_stores:
         copy.wait()
     early_store.wait()
-    result_store.wait()
-    input_store.wait()
 
 
 def run_kernel(tokens, mask, out_grad, vectors, qkv_bias, expand_bias, rel_height, rel_width, sources):
@@ -1177,9 +1201,9 @@
     sds = jax.ShapeDtypeStruct
     any_spec = pl.BlockSpec(memory_space=pl.ANY)
     vmem_spec = pl.BlockSpec(memory_space=pltpu.VMEM)
-    out_shape = [sds((own, width), BF), sds((own, width), F32)]
+    out_shape = [sds(tokens.shape, BF), sds(tokens.shape, F32)]
     out_shape += [sds(source.shape, BF) for source in sources]
-    out_shape += [sds((16, width), F32), sds((8, width), F32), sds((64, LANES), F32)]
+    out_shape += [sds((16, width), F32), sds((16, half), F32), sds((64, LANES), F32)]
     first, second = zip(*[halves(n) for n in rows])
     out_shape += [sds((4, 2, n, half), BF) for n in first]
     out_shape += [sds((4, 2, n, half), BF) for n in second]
@@ -1197,12 +1221,12 @@
     scratch += [vmem((both, width), F32)] * 2
     scratch += [vmem((own, width), F32)] * 3
     scratch += [vmem((both, half), BF), vmem((both, half), BF)]
-    scratch += [vmem((4, 8, width), F32), vmem((16, width), F32), vmem((7, 16, width), F32)]
-    scratch += [vmem((8, width), F32), vmem((7, 8, width), F32)]
-    scratch += [vmem((64, LANES), F32), vmem((7, 64, LANES), F32)]
+    scratch += [vmem((4, 8, width), F32), vmem((16, width), F32), vmem((16, width), F32), vmem((7, 8, width), F32)]
+    scratch += [vmem((16, half), F32), vmem((16, half), F32), vmem((7, 8, half), F32)]
+    scratch += [vmem((64, LANES), F32), vmem((64, LANES), F32), vmem((7, 32, LANES), F32)]
     scratch += [vmem((4, 1, half), F32), vmem((4, 1, qkv_width), F32), vmem((2 * LANES, LANES), F32)]
     scratch += [vmem((2 * LANES, LANES), BF), vmem((3 * LANES, LANES), BF), vmem((2, 32, HEAD), F32)]
-    scratch += [dma((4, 4, 6))] * 2 + [dma((4, 4, 5)), dma((4, 4, 6))] + [dma((4, 5))] * 2 + [dma((41,))] * 2
+    scratch += [dma((4, 4, 6))] * 2 + [dma((4, 4, 5)), dma((4, 4, 6))] + [dma((4, 5))] * 2 + [dma((44,))] * 2
     scratch += [dma((4,))] * 2 + [dma((8,))] * 2 + [dma((11,)), dma((4,))]
     got = pl.pallas_call(
         kernel,
@@ -1220,29 +1244,31 @@
 
 def finish_kernel(early, late, rel, *refs):
     wide, (bias_q, bias_e, height, width_out, rms), rows_out = refs[:6], refs[6:11], refs[11:17]
-    outs, held, full, load, store = refs[17:23], refs[23:29], refs[29:35], refs[35], refs[36]
+    outs, held, full, load, store = refs[17:23], refs[23:29], refs[29:33], refs[33], refs[34]
     z = lax.axis_index("col")
     loads = [pltpu.make_async_copy(src, to, load.at[i]) for i, (src, to) in enumerate(zip(wide, held))]
+    full = list(full) + list(held[4:])
     stores = [pltpu.make_async_copy(src, to, store.at[i]) for i, (src, to) in enumerate(zip(full, outs))]
-    for i in (3, 2, 0, 1, 5, 4):
+    for i in (3, 2, 5, 4, 0, 1):
         loads[i].start()
-    places = ((late, 0), (late, 1), (early, 6), (early, 7), (early, 8), (early, 9))
-    for ref, (source, at) in zip(rows_out, places):
-        ref[...] = source[at, :]
     features = early.shape[1]
+    half = features // 2
+    for ref, at in zip(rows_out[:2], (8, 10)):
+        ref[:half] = late[at, :]
+        ref[half:] = late[at + 1, :]
+    for ref, at in zip(rows_out[2:], (6, 7, 8, 9)):
+        ref[...] = early[at, :]
     lane = lax.broadcasted_iota(jnp.int32, (1, LANES), 1)
     stats = jnp.zeros((1, LANES), F32)
     for i in range(rms.shape[0]):
         stats = jnp.where(lane == i, jnp.sum(early[i : i + 1, :], axis=1, keepdims=True), stats)
     rms[...] = jnp.sqrt(stats / (early[5:6, 0:1] * features))[0, : rms.shape[0]]
-    half = features // 2
     part = bias_q.shape[1] // 2
     bias_e[...] = early[pl.ds(10 + z, 1), :].reshape(features)
-    row = late[pl.ds(2 + z, 1), :]
     for side in range(2):
+        row = late[pl.ds(2 * z + side, 1), :]
         for i in range(2):
-            at = (3 * side + 2 * i) * part
-            bias_q[i : i + 1, side * part : (side + 1) * part] = row[:, at : at + part]
+            bias_q[i : i + 1, side * part : (side + 1) * part] = row[:, 2 * i * part : (2 * i + 1) * part]
     count = height.shape[0]
     turn = lax.broadcasted_iota(jnp.int32, (32, 32), 0) + lax.broadcasted_iota(jnp.int32, (32, 32), 1) == count - 1
     turned = jnp.dot(turn.astype(F32), rel[:32], precision=lax.Precision.HIGHEST, preferred_element_type=F32)
@@ -1258,24 +1284,9 @@
             full[i][at] = held[i][at].astype(F32)
 
         stores[i].start()
-    loads[5].wait()
-
-    @pl.loop(0, SIDE)
-    def _(i):
-        for w in range(2):
-            at = pl.multiple_of(w * WROWS + i * SIDE_PAD, SIDE_PAD)
-            full[5][pl.ds(i * SIDE, SIDE), w, :] = held[5][pl.ds(at, SIDE_PAD)][:SIDE]
-
-    stores[5].start()
-    loads[4].wait()
-
-    @pl.loop(0, SIDE)
-    def _(i):
-        places = [pl.multiple_of(w * WROWS + i * SIDE_PAD, SIDE_PAD) for w in range(2)]
-        some = [held[4][pl.ds(at, SIDE_PAD)][:SIDE].astype(F32) for at in places]
-        full[4][pl.ds(i * SIDE, SIDE)] = jnp.stack(some, axis=1).astype(BF)
-
-    stores[4].start()
+        for j in {3: (5,), 2: (4,)}.get(i, ()):
+            loads[j].wait()
+            stores[j].start()
     for copy in stores:
         copy.wait()
 
@@ -1287,23 +1298,20 @@
     sds = jax.ShapeDtypeStruct
     any_spec = pl.BlockSpec(memory_space=pl.ANY)
     vmem_spec = pl.BlockSpec(memory_space=pltpu.VMEM)
-    windows = got[0].shape[0] // WROWS
     out_shape = [sds((2, 2 * part), F32), sds((width,), F32), sds((2 * SIDE - 1, HEAD), F32)]
     out_shape += [sds((2 * SIDE - 1, HEAD), F32), sds((5,), F32)] + [sds((width,), F32)] * 6
-    held = grads + list(got[:2])
     final = [sds(value.shape, F32) for value in grads]
-    final += [sds((SIDE * SIDE, windows, width), value.dtype) for value in got[:2]]
-    out_shape += final
+    out_shape += final + [sds(value.shape, value.dtype) for value in got[:2]]
     return pl.pallas_call(
         finish_kernel,
         out_shape=out_shape,
         in_specs=[vmem_spec] * 3 + [any_spec] * 6,
         out_specs=[vmem_spec] * 11 + [any_spec] * 6,
-        scratch_shapes=[pltpu.VMEM(value.shape, value.dtype) for value in held + final]
+        scratch_shapes=[pltpu.VMEM(value.shape, value.dtype) for value in grads + list(got[:2]) + final]
         + [pltpu.SemaphoreType.DMA((6,))] * 2,
         compiler_params=pltpu.CompilerParams(vmem_limit_bytes=VMEM_LIMIT),
         name="finish",
-    )(early, late, rel, *held)
+    )(early, late, rel, *grads, *got[:2])
 
 
 VMEM_LIMIT = 64 * 1024 * 1024 - 512 * 1024

time: 305 us -> 300 us (0.984)
  Pallas kernels: 302 us -> 297 us
    pallas_call x1, Pallas kernels: 292 us -> 289 us  [run_kernel(): pl.pallas_call(kernel, out_shape=out_shape, in_specs=[any_spec, vmem_spec...]
where the time goes in v2:
time: 300 us; the launch traced here: 298 us
  Pallas kernels  297 us (99%)
    pallas_call x1, Pallas kernels, run_kernel(): pl.pallas_call(kernel, out_shape=out_shape, in_specs=[any_spec, vmem_spec...  289 us
    pallas_call x1, Pallas kernels, finish_outputs(): pl.pallas_call(finish_kernel, out_shape=out_shape, in_specs=[vmem_spec] *...  8.22 us

profile of v2, /device:TPU:0, one launch (start us, length us, event | category | flops | bytes accessed | tf_op | source)
XLA Modules:
  0.0 297.6 jit_solution(8899846911342722732)
XLA Ops:
  0.7 288.5 %block_step.1 = (bf16[196,2,1280]{2,1,0:T(2,128)(2,1)}, f32[196,2,1280]{2,1,0:T(2,128)}, bf16[3,2,160,640]{3,2,1,0:T(8,128)(2,1)}, bf16[2,2,80,640]{3,2,1,0:T(8,...) custom-call(bf16[196,2,1280]{2,1,0:T(2,128)(2,1)} %bitcast.23, ...), custom_call_target="tpu_custom_call" | custom-call | tf_op jit(solution)/shard_map/block_step/pallas_call | solution.py:1231
  289.2 8.2 %finish.1 = (f32[2,320]{1,0:T(2,128)}, f32[1280]{0:T(1024)}, f32[27,80]{1,0:T(8,128)}, f32[27,80]{1,0:T(8,128)}, f32[5]{0:T(128)}, /*index=5*/f32[1280]{0:T(1024...) custom-call(f32[16,1280]{1,0:T(8,128)} %get-tuple-element.43.early, ...), custom_call_target="tpu_custom_call" | custom-call | tf_op jit(solution)/shard_map/finish/pallas_call | solution.py:1305

commit v3 on v2

--- a/solution.py
+++ b/solution.py
@@ -247,7 +247,7 @@
 
 
 def halves(rows):
-    first = (rows // 2 + 15) // 16 * 16
+    first = (rows // 16 + 1) // 4 * 32
     return first, rows - first
 
 

time: 300 us -> 298 us (level)
  no operation moved by 1% of the time
where the time goes in v3:
time: 298 us; the launch traced here: 296 us
  Pallas kernels  296 us (99%)
    pallas_call x1, Pallas kernels, run_kernel(): pl.pallas_call(kernel, out_shape=out_shape, in_specs=[any_spec, vmem_spec...  287 us
    pallas_call x1, Pallas kernels, finish_outputs(): pl.pallas_call(finish_kernel, out_shape=out_shape, in_specs=[vmem_spec] *...  8.22 us

profile of v3, /device:TPU:0, one launch (start us, length us, event | category | flops | bytes accessed | tf_op | source)
XLA Modules:
  0.0 296.5 jit_solution(1055898912751933806)
XLA Ops:
  0.7 287.4 %block_step.1 = (bf16[196,2,1280]{2,1,0:T(2,128)(2,1)}, f32[196,2,1280]{2,1,0:T(2,128)}, bf16[3,2,160,640]{3,2,1,0:T(8,128)(2,1)}, bf16[2,2,80,640]{3,2,1,0:T(8,...) custom-call(bf16[196,2,1280]{2,1,0:T(2,128)(2,1)} %bitcast.23, ...), custom_call_target="tpu_custom_call" | custom-call | tf_op jit(solution)/shard_map/block_step/pallas_call | solution.py:1231
  288.1 8.2 %finish.1 = (f32[2,320]{1,0:T(2,128)}, f32[1280]{0:T(1024)}, f32[27,80]{1,0:T(8,128)}, f32[27,80]{1,0:T(8,128)}, f32[5]{0:T(128)}, /*index=5*/f32[1280]{0:T(1024...) custom-call(f32[16,1280]{1,0:T(8,128)} %get-tuple-element.43.early, ...), custom_call_target="tpu_custom_call" | custom-call | tf_op jit(solution)/shard_map/finish/pallas_call | solution.py:1305

commit v4 on v3

--- a/solution.py
+++ b/solution.py
@@ -1082,6 +1082,8 @@
             @pl.when(n == 3)
             def _():
                 swap_gh1.start()
+                small_finish(early_sums, 1)
+                small_start(early_sums, 2)
 
         attention_back_slab(
             s, h1, gm, wq, wp, bias_q_of(s), rel_query, rel_back, codes, act, back, bias_q, rel_acc, heads, half, half_done
@@ -1151,8 +1153,6 @@
     reduce_five((3,))
     interleave(xr2, input_grad)
     interleave(h2, block_out)
-    small_finish(early_sums, 1)
-    small_start(early_sums, 2)
     reduce_three(attn, 3)
     reduce_four(attn)
     small_finish(late_sums, 1)

time: 298 us -> 297 us (level)
  no operation moved by 1% of the time
where the time goes in v4:
time: 297 us; the launch traced here: 296 us
  Pallas kernels  295 us (99%)
    pallas_call x1, Pallas kernels, run_kernel(): pl.pallas_call(kernel, out_shape=out_shape, in_specs=[any_spec, vmem_spec...  287 us
    pallas_call x1, Pallas kernels, finish_outputs(): pl.pallas_call(finish_kernel, out_shape=out_shape, in_specs=[vmem_spec] *...  8.22 us

profile of v4, /device:TPU:0, one launch (start us, length us, event | category | flops | bytes accessed | tf_op | source)
XLA Modules:
  0.0 295.6 jit_solution(7669050146440513095)
XLA Ops:
  0.7 286.6 %block_step.1 = (bf16[196,2,1280]{2,1,0:T(2,128)(2,1)}, f32[196,2,1280]{2,1,0:T(2,128)}, bf16[3,2,160,640]{3,2,1,0:T(8,128)(2,1)}, bf16[2,2,80,640]{3,2,1,0:T(8,...) custom-call(bf16[196,2,1280]{2,1,0:T(2,128)(2,1)} %bitcast.23, ...), custom_call_target="tpu_custom_call" | custom-call | tf_op jit(solution)/shard_map/block_step/pallas_call | solution.py:1231
  287.3 8.2 %finish.1 = (f32[2,320]{1,0:T(2,128)}, f32[1280]{0:T(1024)}, f32[27,80]{1,0:T(8,128)}, f32[27,80]{1,0:T(8,128)}, f32[5]{0:T(128)}, /*index=5*/f32[1280]{0:T(1024...) custom-call(f32[16,1280]{1,0:T(8,128)} %get-tuple-element.43.early, ...), custom_call_target="tpu_custom_call" | custom-call | tf_op jit(solution)/shard_map/finish/pallas_call | solution.py:1305
